TPU v7x, 512 devices: a whole 4x4x16 slice. The times are simulated.
512 devices in a mesh: exp: 4 (over x), imp: 32 (over z, core), wk: 4 (over y).
Axes of the slice: x: 4, y: 4, z: 16, core: 2. Of those that a mesh axis runs over, the one named last changes fastest.
Arguments:
- flows: float32 [4, 2048, 4096], P('wk', 'exp', 'imp'), may hold values from 0.0112 to 284, as said below
- importer_factor: float32 [4096, 256], P('imp'), may hold values from -0.5 to 1.5
- week_factor: float32 [4, 256], P('wk'), may hold values from 0 to 1
Outputs:
- exporter_out: float32 [2048, 256], P('exp')
- importer_out: float32 [4096, 256], P('imp')
- week_out: float32 [4, 256], P('wk')
Inputs may be any that keep to these rules, and one draw needn't show every extreme that they name: `flows`: flows are positive.
All inputs are finite; a program needn't handle non-finite values.
Results may differ from a plain program's by a relative error of at most 0.00022.
Values sent between devices are 32-bit elements; how exact they have to be, the bound alone decides.
A program may use at most 64 MiB of HBM per device.

v0:
```python
import jax
import jax.numpy as jnp
from jax import lax
from jax.sharding import PartitionSpec as P

ridge = 0.2
eps = 1e-06
hp = lax.Precision.HIGHEST


def solve_rows(m, g1, g2):
    h = g1 * g2
    lam = ridge * jnp.trace(h) / h.shape[0]
    v = h + lam * jnp.eye(h.shape[0], dtype=jnp.float32)
    chol = jnp.linalg.cholesky(v)
    return jax.scipy.linalg.cho_solve((chol, True), m.T).T


def cross(x):
    return jnp.dot(x.T, x, precision=hp, preferred_element_type=jnp.float32)


def per_device(flows, importer_factor, week_factor):
    row_part = jnp.sum(flows, 2)
    col_part = jnp.sum(flows, 1)
    gram_part = cross(importer_factor)
    row_tot = lax.psum(row_part, "imp")
    col_tot = lax.psum(col_part, "exp")
    grand = lax.psum(jnp.sum(row_part, 1), ("exp", "imp"))
    gram_b = lax.psum(gram_part, "imp")
    gram_c = lax.psum(cross(week_factor), "wk")
    resid = flows - row_tot[:, :, None] * col_tot[:, None, :] / grand[:, None, None]
    inner = jnp.einsum("kij,jr->kir", resid, importer_factor, precision=hp)
    m_a = lax.psum(jnp.sum(inner * week_factor[:, None, :], 0), ("imp", "wk"))
    raw_a = solve_rows(m_a, gram_b, gram_c)
    count_a = raw_a.shape[0] * lax.axis_size("exp")
    squares_a = lax.psum(jnp.sum(raw_a * raw_a, 0), "exp")
    fac_a = raw_a / jnp.sqrt(squares_a / count_a + eps)
    gram_a = lax.psum(cross(fac_a), "exp")
    weighted = fac_a[None, :, :] * week_factor[:, None, :]
    m_b = lax.psum(jnp.einsum("kij,kir->jr", resid, weighted, precision=hp), ("exp", "wk"))
    raw_b = solve_rows(m_b, gram_a, gram_c)
    count_b = raw_b.shape[0] * lax.axis_size("imp")
    squares_b = lax.psum(jnp.sum(raw_b * raw_b, 0), "imp")
    fac_b = raw_b / jnp.sqrt(squares_b / count_b + eps)
    gram_b2 = lax.psum(cross(fac_b), "imp")
    inner = jnp.einsum("kij,jr->kir", resid, fac_b, precision=hp)
    m_c = lax.psum(jnp.sum(inner * fac_a[None, :, :], 1), ("exp", "imp"))
    raw_c = solve_rows(m_c, gram_a, gram_b2)
    count_c = raw_c.shape[0] * lax.axis_size("wk")
    squares_c = lax.psum(jnp.sum(raw_c * raw_c, 0), "wk")
    fac_c = raw_c / jnp.sqrt(squares_c / count_c + eps)
    return (fac_a, fac_b, fac_c)


def solution(mesh):
    in_specs = (P("wk", "exp", "imp"), P("imp", None), P("wk", None))
    out_specs = (P("exp", None), P("imp", None), P("wk", None))
    return jax.shard_map(
        per_device, mesh=mesh, in_specs=in_specs, out_specs=out_specs, check_vma=False
    )
```

profile of v0, /device:TPU:1, one launch (start us, length us, event | category | flops | bytes accessed | tf_op | source)
XLA Modules:
  0.0 1214.9 jit_solution(1570794201280809967)
XLA Ops:
  7.2 0.8 copy-done
  8.1 1.1 fusion.56
  9.3 0.6 copy-done.7
  9.9 0.8 broadcast_multiply_fusion
  10.9 0.7 fusion.52
  11.5 255.1 %psum.98 = f32[]{:T(128)} all-reduce(f32[]{:T(128)} %get-tuple-element.45), channel_id=1, replica_groups=mesh['exp'=4,'imp'=32,'wk'=4] {'exp','imp'}, use_global_device_ids=true, to_apply=%region_12.14 | all-reduce | flops 1 | bytes 8 | tf_op jit(solution)/shard_map/psum | solution.py:29
  266.6 6.0 psum.97
  272.6 51.9 %psum.96 = f32[512]{0:T(512)S(1)} all-reduce(f32[512]{0:T(512)S(1)} %get-tuple-element.43), channel_id=1, replica_groups=mesh['exp'=4,'imp'=32,'wk'=4] {'imp'}, use_global_device_ids=true, to_apply=%region_8.10 | all-reduce | flops 512 | bytes 4096 | tf_op jit(solution)/shard_map/psum | solution.py:27
  324.5 2.1 fusion
  326.7 1.8 select_reduce_fusion.2
  329.3 11.7 cholesky.172
  341.1 9.8 custom-call.34
  351.4 11.7 cholesky.189
  363.4 0.7 compare_reduce_fusion.4
  365.5 4.3 while.3
  365.8 0.6 fusion.83
  366.4 1.3 dynamic-slice.19
  367.8 0.6 fusion.83
  368.5 1.3 dynamic-slice.19
  369.9 19.7 %custom-call.29 = f32[2,128,128]{1,2,0:T(8,128)S(1)} custom-call(f32[2,128,128]{2,1,0:T(8,128)S(1)} %get-tuple-element.11), custom_call_target="InvertDiagBlocksLowerTriangular" | custom-call | tf_op jit(solution)/shard_map/jit(_cho_solve)/triangular_solve | solution.py:16
  389.5 258.0 %all-reduce.12.cloned.1.call-done = f32[256,512]{0,1:T(8,128)} async-done(((f32[256,512]{0,1:T(8,128)}), f32[256,512]{0,1:T(8,128)}) %all-reduce.12.cloned.1.call-update) | async-done | bytes 524304 | tf_op jit(solution)/shard_map/psum | solution.py:34
  647.6 1.4 fusion.9
  649.0 0.6 convolution_subtract_fusion.1
  649.6 0.4 fusion.35
  650.1 0.4 fusion.34
  650.9 0.6 fusion.33
  651.6 8.4 psum.100
  660.0 1.7 fusion.18
  661.9 2.5 fusion.6
  664.4 0.4 all-reduce.18.cloned.1.call-start
  664.9 49.5 %all-reduce.14.cloned.1.call-done = f32[256,256]{0,1:T(8,128)} async-done(((f32[256,256]{0,1:T(8,128)}), f32[256,256]{0,1:T(8,128)}) %all-reduce.14.cloned.1.call-update) | async-done | bytes 262160 | tf_op jit(solution)/shard_map/psum | solution.py:39
  714.4 1.7 select_reduce_fusion.1
  716.9 11.7 cholesky.206
  728.7 9.8 custom-call.35
  739.0 11.7 cholesky.223
  751.0 0.7 compare_reduce_fusion.2
  751.7 0.7 compare_reduce_fusion.3
  753.8 4.5 while.4
  754.0 0.6 fusion.84
  754.6 1.3 dynamic-slice.21
  756.1 0.6 fusion.84
  756.7 1.3 dynamic-slice.21
  758.2 19.7 %custom-call.30 = f32[2,128,128]{1,2,0:T(8,128)S(1)} custom-call(f32[2,128,128]{2,1,0:T(8,128)S(1)} %get-tuple-element.19), custom_call_target="InvertDiagBlocksLowerTriangular" | custom-call | tf_op jit(solution)/shard_map/jit(_cho_solve)/triangular_solve | solution.py:16
  777.9 54.6 %all-reduce.16.cloned.1.call-done = f32[256,128]{1,0:T(8,128)} async-done(((f32[256,128]{1,0:T(8,128)}), f32[256,128]{1,0:T(8,128)}) %all-reduce.16.cloned.1.call-update) | async-done | bytes 131088 | tf_op jit(solution)/shard_map/psum | solution.py:41
  832.5 1.2 fusion.24
  835.0 48.6 %psum.103 = f32[256]{0:T(256)S(1)} all-reduce(f32[256]{0:T(256)S(1)} %multiply_reduce_fusion.1), channel_id=1, replica_groups=mesh['exp'=4,'imp'=32,'wk'=4] {'imp'}, use_global_device_ids=true, to_apply=%region_20.22 | all-reduce | flops 256 | bytes 2048 | tf_op jit(solution)/shard_map/psum | solution.py:44
  883.6 1.2 fusion.49
  884.9 0.8 copy.26
  885.7 1.4 fusion.1
  887.0 247.6 %psum.105 = f32[1,256]{1,0:T(1,128)S(1)} all-reduce(f32[1,256]{1,0:T(1,128)S(1)} %bitcast.167), channel_id=1, replica_groups=mesh['exp'=4,'imp'=32,'wk'=4] {'exp','imp'}, use_global_device_ids=true, to_apply=%region_24.26 | all-reduce | flops 256 | bytes 2048 | tf_op jit(solution)/shard_map/psum | solution.py:48
  1134.6 1.6 select_reduce_fusion
  1137.1 11.7 cholesky.240
  1148.8 9.8 custom-call.36
  1159.1 11.7 cholesky.257
  1171.2 0.7 compare_reduce_fusion
  1171.9 0.6 compare_reduce_fusion.1
  1174.0 4.3 while.5
  1174.0 0.6 fusion.85
  1174.6 1.4 dynamic-slice.23
  1176.2 0.6 fusion.85
  1176.8 1.4 dynamic-slice.23
  1178.3 19.9 %custom-call.31 = f32[2,128,128]{1,2,0:T(8,128)S(1)} custom-call(f32[2,128,128]{2,1,0:T(8,128)S(1)} %get-tuple-element.27), custom_call_target="InvertDiagBlocksLowerTriangular" | custom-call | tf_op jit(solution)/shard_map/jit(_cho_solve)/triangular_solve | solution.py:16
  1199.4 7.8 psum.106
  1207.2 0.6 rsqrt_multiply_fusion
  (117 shorter events, 7.7 us)
Async XLA Ops:
  7.2 0.9 copy-start
  7.2 319.4 %all-reduce.8.cloned.1.call-start = ((), (), s32[]{:S(2)}) async-start(), calls=%async_computation | async-start | bytes 524288 | tf_op jit(solution)/shard_map/psum | solution.py:30
  9.2 0.7 copy-start.7
  9.2 317.4 %all-reduce.10.cloned.1.call-start = ((), (), s32[]{:S(2)}) async-start(), calls=%async_computation.1 | async-start | bytes 524288 | tf_op jit(solution)/shard_map/psum | solution.py:31
  9.9 0.9 copy-start.5
  10.8 636.8 %all-reduce.12.cloned.1.call-start = ((), (), s32[]{:S(2)}) async-start(), calls=%async_computation.2 | async-start | bytes 1048576 | tf_op jit(solution)/shard_map/psum | solution.py:34
  326.5 387.9 %all-reduce.14.cloned.1.call-start = ((), (), s32[]{:S(2)}) async-start(), calls=%async_computation.3 | async-start | bytes 524288 | tf_op jit(solution)/shard_map/psum | solution.py:39
  647.6 1.5 copy-start.4
  661.8 170.7 %all-reduce.16.cloned.1.call-start = ((), (), s32[]{:S(2)}) async-start(), calls=%async_computation.4 | async-start | bytes 262144 | tf_op jit(solution)/shard_map/psum | solution.py:41
  661.9 223.8 %copy-start.3 = (f32[512,256]{1,0:T(8,128)}, f32[512,256]{1,0:T(8,128)S(1)}, u32[]{:S(2)}) copy-start(f32[512,256]{1,0:T(8,128)S(1)} %fusion.20) | copy-start | bytes 1572868
  661.9 52.5 %copy-start.1 = (f32[256,256]{0,1:T(8,128)S(1)}, f32[256,256]{0,1:T(8,128)}, u32[]{:S(2)}) copy-start(f32[256,256]{0,1:T(8,128)} %all-reduce.10.cloned.1.call-done) | copy-start | bytes 786436
  664.4 470.2 %all-reduce.18.cloned.1.call-start = ((), (), s32[]{:S(2)}) async-start(), calls=%async_computation.5 | async-start | bytes 524288 | tf_op jit(solution)/shard_map/psum | solution.py:46
  832.5 1.2 copy-start.6
  885.7 248.9 %copy-start.2 = (f32[256,256]{0,1:T(8,128)S(1)}, f32[256,256]{0,1:T(8,128)}, u32[]{:S(2)}) copy-start(f32[256,256]{0,1:T(8,128)} %all-reduce.14.cloned.1.call-done) | copy-start | bytes 786436
Sparse Core Ops, SparseCore 0:
  10.3 211.5 all-reduce.7
  224.3 54.7 all-reduce.9
  326.7 320.8 all-reduce.11
  661.9 52.4 all-reduce.13
  718.0 114.3 all-reduce.15
  885.0 204.4 all-reduce.17
where the time goes:
time: 1230 us; the launch traced here: 1210 us
  blocking collectives  625 us (51%)
  waiting for transfers between devices  362 us (29%)
  other arithmetic  170 us (14%)
  between operations  20.7 us (2%)
  matrix products  18.6 us (2%)
  local copies, waits for them, and re-layouts  16.4 us (1%)
    psum x1, waiting for transfers between devices, per_device(): m_a = lax.psum(jnp.sum(inner * week_factor[:, None, :], 0), ('imp', 'wk'))  258 us
    psum x1, blocking collectives, per_device(): grand = lax.psum(jnp.sum(row_part, 1), ('exp', 'imp'))  255 us
    psum x1, blocking collectives, per_device(): m_c = lax.psum(jnp.sum(inner * fac_a[None, :, :], 1), ('exp', 'imp'))  248 us
    another operation x20, other arithmetic, solve_rows(): chol = jnp.linalg.cholesky(v)  103 us
    another operation x8, other arithmetic, solve_rows(): return jax.scipy.linalg.cho_solve((chol, True), m.T).T  59.3 us
    psum x1, waiting for transfers between devices, per_device(): lax.psum(jnp.einsum('kij,kir->jr', resid, weighted, precision=hp), ('exp'...  54.6 us
    psum x1, blocking collectives, per_device(): row_tot = lax.psum(row_part, 'imp')  51.9 us
    psum x1, waiting for transfers between devices, per_device(): gram_a = lax.psum(cross(fac_a), 'exp')  49.5 us
  transfers between devices with their start and end apart: 6, of which 3 were waited for; matrix products, arithmetic and copies ran while one was open for 11% of the time, Pallas kernels for 0%

commit v1 on v0

v1 whole, which is shorter than its diff:
```python
import functools

import jax
import jax.numpy as jnp
from jax import lax
from jax.experimental import pallas as pl
from jax.experimental.pallas import tpu as pltpu
from jax.sharding import PartitionSpec as P

ridge = 0.2
eps = 1e-06
hp = lax.Precision.HIGHEST
f32 = jnp.float32
bf16 = jnp.bfloat16
R = 256
H = 128
MESH = pl.DeviceIdType.MESH
STATS = 4
STEPS = 7


def dot(a, b, ca=1, cb=0):
    return lax.dot_general(a, b, (((ca,), (cb,)), ((), ())), precision=hp, preferred_element_type=f32)


def split(a):
    hi = a.astype(bf16)
    return hi, (a - hi.astype(f32)).astype(bf16)


def dot3(a, b):
    ah, al = a
    bh, bl = b
    d = functools.partial(jnp.dot, preferred_element_type=f32)
    return d(ah, bh) + (d(ah, bl) + d(al, bh))


def eye():
    return (lax.broadcasted_iota(jnp.int32, (R, R), 0) == lax.broadcasted_iota(jnp.int32, (R, R), 1)).astype(f32)


def inverse_start(h, diag_sum):
    lam = ridge * diag_sum / R
    one = eye()
    v = h + lam * one
    top = 1.0 + R / ridge
    alpha = 2.0 / (lam * (1.0 + top))
    delta = (top - 1.0) / (top + 1.0)
    e = one - alpha * v
    x = None
    return [v, e, x, alpha, delta, one]


def inverse_steps(state, n):
    v, e, x, alpha, delta, one = state
    for _ in range(n):
        c = 2.0 / (2.0 - delta * delta)
        delta = delta * delta / (2.0 - delta * delta)
        se = split(e)
        if x is None:
            x = (c * alpha) * (one + e)
        else:
            x = c * (x + dot3(split(x), se))
        e = c * dot3(se, se) + (1.0 - c) * one
    return [v, e, x, alpha, delta, one]


def inverse_end(state):
    v, e, x, alpha, delta, one = state
    for _ in range(2):
        r = one - dot(v, x)
        x = x + dot3(split(x), split(r))
    return x


def kernel(ne, nz, nk, f_ref, b_ref, w_ref, a_out, b_out, c_out,
           u, c_in, y_in, z_in, ma, cx, wx,
           cs, ci, zs, zi, za, xs, ax, ag, mbp, mi, mo, res,
           ssem, rsem):
    e = lax.axis_index("exp")
    p = lax.axis_index("imp")
    k = lax.axis_index("wk")
    z = lax.div(p, 2)
    c = lax.rem(p, 2)
    o = 1 - c
    nq = ne * nk
    q = e * nk + k
    ri = f_ref.shape[1]
    rj = f_ref.shape[2]
    gs = R // nq
    cr = gs // nz
    yc = ri // nk
    zc = yc // nz
    jc = rj // nq
    used = [0]
    pending = []

    def take(n):
        base = used[0]
        used[0] += n
        return base

    def remote(src, dst, s, dev):
        return pltpu.make_async_remote_copy(
            src_ref=src, dst_ref=dst, send_sem=ssem.at[s], recv_sem=rsem.at[s],
            device_id=dev, device_id_type=MESH)

    core_dev = {"imp": z * 2 + o}

    def push_core(src, dst):
        cp = remote(src, dst, take(1), core_dev)
        cp.start()
        pending.append(cp.wait_send)
        return cp.wait_recv

    def push_group(n, dev, src, dst, back):
        base = take(n)

        def go(d, carry):
            remote(src(d), dst, base + d, dev(d)).start()
            return carry

        def sent(d, carry):
            remote(src(d), dst, base + d, dev(d)).wait_send()
            return carry

        def arrived(d, carry):
            remote(back(d), back(d), base + d, dev(d)).wait_recv()
            return carry

        lax.fori_loop(1, n, go, 0)
        pending.append(lambda: lax.fori_loop(1, n, sent, 0))
        return lambda: lax.fori_loop(1, n, arrived, 0)

    def zto(d):
        return lax.rem(z + d, nz)

    def zfrom(d):
        return lax.rem(z - d + nz, nz)

    def zdev(d):
        return {"imp": zto(d) * 2 + c}

    def yto(d):
        return lax.rem(k + d, nk)

    def yfrom(d):
        return lax.rem(k - d + nk, nk)

    def ydev(d):
        return {"wk": yto(d)}

    def xto(d):
        return lax.rem(e + d, ne)

    def xfrom(d):
        return lax.rem(e - d + ne, ne)

    def xdev(d):
        return {"exp": xto(d)}

    def qto(d):
        return lax.rem(q + d, nq)

    def qfrom(d):
        return lax.rem(q - d + nq, nq)

    def qdev(d):
        return {"exp": lax.div(qto(d), nk), "wk": lax.rem(qto(d), nk)}

    barrier = pltpu.get_barrier_semaphore()
    pl.semaphore_signal(barrier, inc=1, device_id=core_dev, device_id_type=MESH)

    def greet_z(d, carry):
        pl.semaphore_signal(barrier, inc=1, device_id=zdev(d), device_id_type=MESH)
        return carry

    def greet_q(d, carry):
        pl.semaphore_signal(barrier, inc=1, device_id=qdev(d), device_id_type=MESH)
        return carry

    lax.fori_loop(1, nz, greet_z, 0)
    lax.fori_loop(1, nq, greet_q, 0)

    def chain_fill(n, gram, stats):
        for h in range(2):
            u_g = gram[:, h * H:(h + 1) * H]
            mbp[h, :, :] = u_g
            cs[n, h, pl.ds(0, gs), :] = mbp[h, pl.ds(pl.multiple_of(q * gs, gs), gs), :]
            for s, row in enumerate(stats):
                cs[n, h, gs + s:gs + s + 1, :] = row[:, h * H:(h + 1) * H]
            for s in range(len(stats), STATS):
                cs[n, h, gs + s:gs + s + 1, :] = jnp.zeros((1, H), f32)

    def chain_core(n):
        return push_core(cs.at[n, o], ci.at[n])

    def chain_z1(n):
        t = cs[n, c] + ci[n]
        for i in range(nz):
            zs[n, i, 0:cr, :] = t[i * cr:(i + 1) * cr]
            s = gs + i % STATS
            zs[n, i, cr:cr + 1, :] = t[s:s + 1]
        zi[n, z, :, :] = zs[n, z]
        return push_group(nz, zdev, lambda d: zs.at[n, zto(d)], zi.at[n, z], lambda d: zi.at[n, zfrom(d)])

    def chain_z2(n):
        za[n, z, :, :] = jnp.sum(zi[n], axis=0)
        return push_group(nz, zdev, lambda d: za.at[n, z], za.at[n, z], lambda d: za.at[n, zfrom(d)])

    def chain_q(n):
        for i in range(nz):
            xs[n, c, q, i * cr:(i + 1) * cr, :] = za[n, i, 0:cr, :]
        for s in range(STATS):
            xs[n, c, q, gs + s:gs + s + 1, :] = za[n, s, cr:cr + 1, :]
        return push_group(nq, qdev, lambda d: xs.at[n, c, q], xs.at[n, c, q], lambda d: xs.at[n, c, qfrom(d)])

    def chain_back(n):
        return push_core(xs.at[n, c], xs.at[n, c])

    def chain_gram(n):
        return jnp.concatenate([xs[n, h, :, 0:gs, :].reshape(R, H) for h in range(2)], axis=1)

    def chain_stat(n, qq, s):
        return jnp.concatenate([xs[n, h, qq, gs + s:gs + s + 1, :] for h in range(2)], axis=1)

    def chain_week(n, kk, s):
        tot = chain_stat(n, kk, s)
        for ee in range(1, ne):
            tot = tot + chain_stat(n, ee * nk + kk, s)
        return tot

    f = f_ref[0]
    b = b_ref[...]
    w = w_ref[...]
    rowp = dot(jnp.ones((8, rj), f32), f, 1, 1)
    colp = jnp.sum(f, axis=0, keepdims=True)
    g = dot(f, b - 0.5)
    v = jnp.sum(g, axis=0, keepdims=True)
    gw = g * w
    u[0, :, :] = gw[:, 0:H]
    u[1, :, :] = gw[:, H:R]
    rows = [rowp[0:1, i * R:(i + 1) * R] for i in range(ri // R)]
    chain_fill(0, dot(b, b, 0, 0), [v, jnp.concatenate([colp, jnp.zeros((1, R - rj), f32)], axis=1)] + rows)
    cx[e, :, :] = colp
    wx[k, :, :] = w

    pl.semaphore_wait(barrier, 1 + (nz - 1) + (nq - 1))

    w_cs = chain_core(0)
    w_u = push_core(u.at[o], c_in)
    w_w = push_group(nk, ydev, lambda d: wx.at[k], wx.at[k], lambda d: wx.at[yfrom(d)])
    w_c = push_group(ne, xdev, lambda d: cx.at[e], cx.at[e], lambda d: cx.at[xfrom(d)])

    w_cs()
    w_z1 = chain_z1(0)
    w_u()
    u[c, :, :] = u[c] + c_in[...]
    y_in[k, :, :] = u[c, pl.ds(pl.multiple_of(k * yc, yc), yc), :]
    w_y = push_group(nk, ydev, lambda d: u.at[c, pl.ds(pl.multiple_of(yto(d) * yc, yc), yc)],
                     y_in.at[k], lambda d: y_in.at[yfrom(d)])
    w_z1()
    w_z2 = chain_z2(0)
    w_y()
    y_in[0, :, :] = jnp.sum(y_in[...], axis=0)
    z_in[z, :, :] = y_in[0, pl.ds(pl.multiple_of(z * zc, zc), zc), :]
    w_z3 = push_group(nz, zdev, lambda d: y_in.at[0, pl.ds(pl.multiple_of(zto(d) * zc, zc), zc)],
                      z_in.at[z], lambda d: z_in.at[zfrom(d)])
    w_z2()
    w_q = chain_q(0)

    def tile(zz):
        return ma.at[c, pl.ds(pl.multiple_of(k * yc + zz * zc, zc), zc)]

    def part(kk):
        return ma.at[c, pl.ds(pl.multiple_of(kk * yc, yc), yc)]

    w_z3()
    tile(z)[...] = jnp.sum(z_in[...], axis=0)
    w_z4 = push_group(nz, zdev, lambda d: tile(z), tile(z), lambda d: tile(zfrom(d)))
    w_w()
    ws = jnp.concatenate([wx[i] for i in range(nk)] + [jnp.zeros((8 - nk, R), f32)], axis=0)
    gram_c = dot(ws, ws, 0, 0)
    w_q()
    w_b = chain_back(0)
    w_z4()
    w_y2 = push_group(nk, ydev, lambda d: part(k), part(k), lambda d: part(yfrom(d)))
    w_b()
    h1 = chain_gram(0) * gram_c
    one = eye()
    inv = inverse_steps(inverse_start(h1, jnp.sum(h1 * one)), 3)
    w_y2()
    w_m = push_core(ma.at[c], ma.at[c])

    w_c()
    col = cx[0]
    for i in range(1, ne):
        col = col + cx[i]
    zero = jnp.zeros((1, R), f32)
    coef, totals = [], []
    for kk in range(nk):
        grand = jnp.sum(chain_week(0, kk, 1))
        coef.append(chain_week(0, kk, 0) * ws[kk:kk + 1] / grand)
        totals.append(jnp.concatenate([chain_stat(0, e * nk + kk, 2 + i) for i in range(ri // R)], axis=1))
    coef = jnp.concatenate(coef + [zero] * (8 - nk), axis=0)
    totals = jnp.concatenate(totals + [jnp.zeros((1, ri), f32)] * (8 - nk), axis=0)
    mine = (lax.broadcasted_iota(jnp.int32, (8, 1), 0) == k).astype(f32)
    grand = jnp.zeros((1, 1), f32)
    for ee in range(ne):
        grand = grand + jnp.sum(chain_stat(0, ee * nk + k, 1), axis=1, keepdims=True)
    res[...] = f - dot(totals * mine, (col / grand) * mine, 0, 0)

    inv = inverse_steps(inv, STEPS - 3)
    x1 = inverse_end(inv)
    w_m()
    m_a = jnp.concatenate([ma[0], ma[1]], axis=1) - dot(totals, coef, 0, 0)
    raw_a = dot(m_a, x1)
    a_out[...] = raw_a

    gram = dot(raw_a, raw_a, 0, 0)
    mbp[0, :, :] = gram[:, 0:H]
    mbp[1, :, :] = gram[:, H:R]
    gr = R // nk
    ax[e, :, :] = mbp[c, pl.ds(pl.multiple_of(k * gr, gr), gr), :]
    w_ax = push_group(ne, xdev, lambda d: ax.at[e], ax.at[e], lambda d: ax.at[xfrom(d)])

    t = dot(res[...], raw_a, 0, 0)
    tw = t * w
    for i in range(nq):
        mo[0, i, :, :] = tw[i * jc:(i + 1) * jc]
    mi[q, :, :] = mo[0, q]
    w_mi = push_group(nq, qdev, lambda d: mo.at[0, qto(d)], mi.at[q], lambda d: mi.at[qfrom(d)])

    def gpart(kk):
        return ag.at[c, pl.ds(pl.multiple_of(kk * gr, gr), gr)]

    w_ax()
    gpart(k)[...] = jnp.sum(ax[...], axis=0)
    w_ag = push_group(nk, ydev, lambda d: gpart(k), gpart(k), lambda d: gpart(yfrom(d)))
    w_mi()
    mo[1, q, :, :] = jnp.sum(mi[...], axis=0)
    w_mo = push_group(nq, qdev, lambda d: mo.at[1, q], mo.at[1, q], lambda d: mo.at[1, qfrom(d)])
    w_ag()
    w_ac = push_core(ag.at[c], ag.at[c])
    w_ac()
    gram_a = jnp.concatenate([ag[0], ag[1]], axis=1)

    def unscale(gram, count):
        d = gram * one
        inv_row = 1.0 / jnp.sqrt(jnp.sum(d, axis=0, keepdims=True) / count + eps)
        inv_col = 1.0 / jnp.sqrt(jnp.sum(d, axis=1, keepdims=True) / count + eps)
        return inv_row, gram * inv_row * inv_col

    sa, gram_a = unscale(gram_a, ri * ne)
    h2 = gram_a * gram_c
    inv = inverse_steps(inverse_start(h2, jnp.sum(h2 * one)), STEPS)
    x2 = inverse_end(inv)
    a_out[...] = a_out[...] * sa
    w_mo()
    m_b = mo[1].reshape(rj, R) * sa
    raw_b = dot(m_b, x2)

    chain_fill(1, dot(raw_b, raw_b, 0, 0), [jnp.sum(t * raw_b, axis=0, keepdims=True)])
    w_cs = chain_core(1)
    w_cs()
    w_z1 = chain_z1(1)
    w_z1()
    w_z2 = chain_z2(1)
    w_z2()
    w_q = chain_q(1)
    w_q()
    w_b = chain_back(1)
    w_b()
    sb, gram_b2 = unscale(chain_gram(1), rj * nz * 2)
    b_out[...] = raw_b * sb
    h3 = gram_a * gram_b2
    inv = inverse_steps(inverse_start(h3, jnp.sum(h3 * one)), STEPS)
    x3 = inverse_end(inv)
    m_c = jnp.concatenate([chain_week(1, kk, 0) * sa * sb for kk in range(nk)] + [zero] * (8 - nk), axis=0)
    raw_c = dot(m_c, x3)
    sc = jnp.sqrt(jnp.sum(raw_c * raw_c, axis=0, keepdims=True) / nk + eps)
    c_out[...] = jnp.sum(raw_c * mine, axis=0, keepdims=True) / sc

    for fin in pending:
        fin()


def per_device(ne, nz, nk, flows, importer_factor, week_factor):
    ri, rj = flows.shape[1], flows.shape[2]
    nq = ne * nk
    gs = R // nq
    cr = gs // nz
    yc = ri // nk
    vm = functools.partial(pltpu.VMEM, dtype=f32)
    nsem = 512
    return pl.pallas_call(
        functools.partial(kernel, ne, nz, nk),
        out_shape=(
            jax.ShapeDtypeStruct((ri, R), f32),
            jax.ShapeDtypeStruct((rj, R), f32),
            jax.ShapeDtypeStruct((1, R), f32),
        ),
        in_specs=[pl.BlockSpec(memory_space=pltpu.VMEM)] * 3,
        out_specs=[pl.BlockSpec(memory_space=pltpu.VMEM)] * 3,
        scratch_shapes=[
            vm((2, ri, H)),
            vm((ri, H)),
            vm((nk, yc, H)),
            vm((nz, yc // nz, H)),
            vm((2, ri, H)),
            vm((ne, 1, rj)),
            vm((nk, 1, R)),
            vm((2, 2, gs + STATS, H)),
            vm((2, gs + STATS, H)),
            vm((2, nz, cr + 1, H)),
            vm((2, nz, cr + 1, H)),
            vm((2, nz, cr + 1, H)),
            vm((2, 2, nq, gs + STATS, H)),
            vm((ne, R // nk, H)),
            vm((2, R, H)),
            vm((2, R, H)),
            vm((nq, rj // nq, R)),
            vm((2, nq, rj // nq, R)),
            vm((ri, rj)),
            pltpu.SemaphoreType.DMA((nsem,)),
            pltpu.SemaphoreType.DMA((nsem,)),
        ],
        compiler_params=pltpu.CompilerParams(
            collective_id=0, has_side_effects=True, vmem_limit_bytes=48 * 1024 * 1024
        ),
    )(flows, importer_factor, week_factor)


def solution(mesh):
    in_specs = (P("wk", "exp", "imp"), P("imp", None), P("wk", None))
    out_specs = (P("exp", None), P("imp", None), P("wk", None))
    fn = functools.partial(per_device, mesh.shape["exp"], mesh.shape["imp"] // 2, mesh.shape["wk"])
    return jax.shard_map(fn, mesh=mesh, in_specs=in_specs, out_specs=out_specs, check_vma=False)
```

time: 1230 us -> 108 us (0.09); the launches traced: 1210 us -> 108 us
  blocking collectives: 625 us -> 0 us
  waiting for transfers between devices: 362 us -> 0 us
  other arithmetic: 170 us -> 0 us
  Pallas kernels: 0 us -> 103 us
  between operations: 20.7 us -> 0.65 us
  matrix products: 18.6 us -> 0 us
    psum x7 -> x0, blocking collectives: 625 us -> none  [the longest x1 255 us: per_device(): grand = lax.psum(jnp.sum(row_part, 1), ('exp', 'imp'))]
    psum x6 -> x0, waiting for transfers between devices: 362 us -> none  [the longest x1 258 us: per_device(): m_a = lax.psum(jnp.sum(inner * week_factor[:, None, :], 0), ('imp', 'wk'))]
    another operation x28 -> x0, other arithmetic: 163 us -> none  [the longest x20 103 us: solve_rows(): chol = jnp.linalg.cholesky(v)]
    pallas_call x0 -> x1, Pallas kernels: none -> 103 us  [per_device(): pl.pallas_call(functools.partial(kernel, ne, nz, nk), out_shape=(jax.Shap...]
    another operation x53 -> x0, local copies, waits for them, and re-layouts: 13.6 us -> none
  transfers between devices with their start and end apart: 6 -> 0, of which waited for: 3 -> 0; matrix products, arithmetic and copies ran while one was open for 11% -> 0% of each run, Pallas kernels for 0% -> 0%
where the time goes in v1:
time: 108 us
  Pallas kernels  103 us (95%)
  local copies, waits for them, and re-layouts  4.54 us (4%)
    pallas_call x1, Pallas kernels, per_device(): pl.pallas_call(functools.partial(kernel, ne, nz, nk), out_shape=(jax.Shap...  103 us
    unnamed x9, local copies, waits for them, and re-layouts  4.54 us

profile of v1, /device:TPU:1, one launch (start us, length us, event | category | flops | bytes accessed | tf_op | source)
XLA Modules:
  0.0 108.2 jit_solution(4898088431581127803)
XLA Ops:
  0.6 0.0 copy-start
  0.6 0.9 copy-done
  1.6 0.0 copy-start.1
  1.6 0.9 copy-done.1
  2.5 0.0 copy-start.2
  2.5 0.7 copy-done.2
  3.2 103.0 %shard_map.58 = (f32[512,256]{1,0:T(8,128)S(1)}, f32[128,256]{1,0:T(8,128)S(1)}, f32[1,256]{1,0:T(1,128)S(1)}) custom-call(f32[1,512,128]{2,1,0:T(8,128)S(1)} %copy-done, f32[128,256]{1,0:T(8,128)S(1)} %copy-done.1, f32[1,256]{1,0:T(1,128)S(1)} %copy-done.2), custom_call_target="tpu_custom_call" | custom-call | tf_op jit(solution)/shard_map/pallas_call | solution.py:396
  106.2 0.8 copy.9
  107.0 0.7 copy.10
  107.6 0.6 copy.11
Async XLA Ops:
  0.6 1.0 copy-start
  1.6 0.9 copy-start.1
  2.5 0.7 copy-start.2

commit v2 on v1

v2 whole, which is shorter than its diff:
```python
import functools

import jax
import jax.numpy as jnp
from jax import lax
from jax.experimental import pallas as pl
from jax.experimental.pallas import tpu as pltpu
from jax.sharding import PartitionSpec as P

ridge = 0.2
eps = 1e-06
hp = lax.Precision.HIGHEST
f32 = jnp.float32
bf16 = jnp.bfloat16
R = 256
H = 128
MESH = pl.DeviceIdType.MESH
STATS = 5
STEPS = 7


def dot(a, b, ca=1, cb=0):
    return lax.dot_general(a, b, (((ca,), (cb,)), ((), ())), precision=hp, preferred_element_type=f32)


def split(a):
    hi = a.astype(bf16)
    return hi, (a - hi.astype(f32)).astype(bf16)


def dot3(a, b):
    ah, al = a
    bh, bl = b
    d = functools.partial(jnp.dot, preferred_element_type=f32)
    return d(ah, bh) + (d(ah, bl) + d(al, bh))


def eye():
    return (lax.broadcasted_iota(jnp.int32, (R, R), 0) == lax.broadcasted_iota(jnp.int32, (R, R), 1)).astype(f32)


def inverse_start(h, diag_sum):
    lam = ridge * diag_sum / R
    one = eye()
    v = h + lam * one
    top = 1.0 + R / ridge
    alpha = 2.0 / (lam * (1.0 + top))
    delta = (top - 1.0) / (top + 1.0)
    e = one - alpha * v
    x = None
    return [v, e, x, alpha, delta, one]


def inverse_steps(state, n):
    v, e, x, alpha, delta, one = state
    for _ in range(n):
        c = 2.0 / (2.0 - delta * delta)
        delta = delta * delta / (2.0 - delta * delta)
        se = split(e)
        if x is None:
            x = (c * alpha) * (one + e)
        else:
            x = c * (x + dot3(split(x), se))
        e = c * dot3(se, se) + (1.0 - c) * one
    return [v, e, x, alpha, delta, one]


def inverse_end(state):
    v, e, x, alpha, delta, one = state
    for _ in range(2):
        r = one - dot(v, x)
        x = x + dot3(split(x), split(r))
    return x


def triangle():
    r = lax.broadcasted_iota(jnp.int32, (H, H), 0)
    c = lax.broadcasted_iota(jnp.int32, (H, H), 1)
    return r, c


def pack(g):
    r, c = triangle()
    g11 = g[H:, H:]
    return jnp.where(r <= c, g[:H, :H], g11), g[:H, H:], jnp.sum(jnp.where(r == c, g11, 0.0), axis=0, keepdims=True)


def unpack(p0, p1, d):
    r, c = triangle()
    g00 = jnp.where(r <= c, p0, 0.0) + jnp.where(r < c, p0, 0.0).T
    low = jnp.where(r > c, p0, 0.0)
    g11 = low + low.T + jnp.where(r == c, d, 0.0)
    return jnp.concatenate(
        [jnp.concatenate([g00, p1], axis=1), jnp.concatenate([p1.T, g11], axis=1)], axis=0)


def kernel(ne, nz, nk, f_hbm, b_hbm, w_hbm, a_out, b_out, c_out,
           f_ref, b_ref, w_ref, fa, u, c_in, z_in, ma, cq, wx,
           pk, cs, ci, zi, xs, gi, gx, gag, mi, mo, mos, res, raw,
           ssem, rsem, lsem):
    e = lax.axis_index("exp")
    p = lax.axis_index("imp")
    k = lax.axis_index("wk")
    z = lax.div(p, 2)
    c = lax.rem(p, 2)
    o = 1 - c
    nq = ne * nk
    q = e * nk + k
    ri, rj = f_ref.shape
    yc = ri // nk
    zc = yc // nz
    jc = rj // nq
    gs = H // nq
    used = [0]
    pending = []

    loads = [pltpu.make_async_copy(f_hbm.at[0], f_ref, lsem.at[0]),
             pltpu.make_async_copy(b_hbm, b_ref, lsem.at[1]),
             pltpu.make_async_copy(w_hbm, w_ref, lsem.at[2])]
    for cp in loads:
        cp.start()

    def take():
        used[0] += 1
        return used[0] - 1

    def remote(src, dst, s, dev):
        return pltpu.make_async_remote_copy(
            src_ref=src, dst_ref=dst, send_sem=ssem.at[s], recv_sem=rsem.at[s],
            device_id=dev, device_id_type=MESH)

    core_dev = {"imp": z * 2 + o}

    def push_core(src, dst):
        cp = remote(src, dst, take(), core_dev)
        cp.start()
        pending.append(cp.wait_send)
        return cp.wait_recv

    def push_group(n, dev, src, dst, every):
        s = take()

        def go(d, carry):
            remote(src(d), dst, s, dev(d)).start()
            return carry

        lax.fori_loop(1, n, go, 0)
        cp = remote(every, every, s, dev(1))
        pending.append(cp.wait_send)
        return cp.wait_recv

    def zto(d):
        return lax.rem(z + d, nz)

    def zdev(d):
        return {"imp": zto(d) * 2 + c}

    def yto(d):
        return lax.rem(k + d, nk)

    def ydev(d):
        return {"wk": yto(d)}

    def qto(d):
        return lax.rem(q + d, nq)

    def qdev(d):
        return {"exp": lax.div(qto(d), nk), "wk": lax.rem(qto(d), nk)}

    barrier = pltpu.get_barrier_semaphore()
    pl.semaphore_signal(barrier, inc=1, device_id=core_dev, device_id_type=MESH)

    def greet_z(d, carry):
        pl.semaphore_signal(barrier, inc=1, device_id=zdev(d), device_id_type=MESH)
        return carry

    def greet_q(d, carry):
        pl.semaphore_signal(barrier, inc=1, device_id=qdev(d), device_id_type=MESH)
        return carry

    lax.fori_loop(1, nz, greet_z, 0)
    lax.fori_loop(1, nq, greet_q, 0)

    def chain_fill(n, gram, stats):
        p0, p1, d = pack(gram)
        pk[0, :, :] = p0
        pk[1, :, :] = p1
        for h in range(2):
            cs[n, h, 0:gs, :] = pk[h, pl.ds(pl.multiple_of(q * gs, gs), gs), :]
            cs[n, h, gs:gs + 1, :] = d
            for s, row in enumerate(stats):
                cs[n, h, gs + 1 + s:gs + 2 + s, :] = row[:, h * H:(h + 1) * H]
            for s in range(len(stats), STATS - 1):
                cs[n, h, gs + 1 + s:gs + 2 + s, :] = jnp.zeros((1, H), f32)

    def chain_core(n):
        return push_core(cs.at[n, o], ci.at[n])

    def chain_z(n):
        zi[n, z, :, :] = cs[n, c] + ci[n]
        return push_group(nz, zdev, lambda d: zi.at[n, z], zi.at[n, z], zi.at[n, pl.ds(0, nz - 1)])

    def chain_q(n):
        xs[n, c, q, :, :] = jnp.sum(zi[n], axis=0)
        return push_group(nq, qdev, lambda d: xs.at[n, c, q], xs.at[n, c, q], xs.at[n, c, pl.ds(0, nq - 1)])

    def chain_back(n):
        return push_core(xs.at[n, c], xs.at[n, c])

    def chain_gram(n):
        return unpack(xs[n, 0, :, 0:gs, :].reshape(H, H), xs[n, 1, :, 0:gs, :].reshape(H, H), xs[n, 0, 0, gs:gs + 1, :])

    def chain_stat(n, qq, s):
        return jnp.concatenate([xs[n, h, qq, gs + 1 + s:gs + 2 + s, :] for h in range(2)], axis=1)

    def add(terms):
        tot = terms[0]
        for term in terms[1:]:
            tot = tot + term
        return tot

    for cp in loads:
        cp.wait()
    f = f_ref[...]
    b = b_ref[...]
    w = w_ref[...]
    shifted = b - 0.5
    wx[k, :, :] = w
    rowp = dot(jnp.ones((8, rj), f32), f, 1, 1)
    colp = jnp.sum(f, axis=0, keepdims=True)
    cq[q, :, :] = colp
    v = dot(jnp.broadcast_to(colp, (8, rj)), shifted)[0:1]
    chain_fill(0, dot(b, b, 0, 0), [v] + [rowp[0:1, i * R:(i + 1) * R] for i in range(ri // R)])
    fa[k, :, :] = f_ref[pl.ds(pl.multiple_of(k * yc, yc), yc), :]

    pl.semaphore_wait(barrier, 1 + (nz - 1) + (nq - 1))

    w_f = push_group(nk, ydev, lambda d: f_ref.at[pl.ds(pl.multiple_of(yto(d) * yc, yc), yc)], fa.at[k], fa.at[pl.ds(0, nk - 1)])
    w_cs = chain_core(0)
    w_w = push_group(nk, ydev, lambda d: wx.at[k], wx.at[k], wx.at[pl.ds(0, nk - 1)])
    w_cs()
    w_z = chain_z(0)
    w_c = push_group(nq, qdev, lambda d: cq.at[q], cq.at[q], cq.at[pl.ds(0, nq - 1)])

    w_w()
    ws = jnp.concatenate([wx[i] for i in range(nk)] + [jnp.zeros((8 - nk, R), f32)], axis=0)
    gram_c = dot(ws, ws, 0, 0)
    w_f()
    g = dot(fa[...].reshape(ri, rj), shifted)
    gw = add([g[i * yc:(i + 1) * yc] * ws[i:i + 1] for i in range(nk)])
    u[0, :, :] = gw[:, 0:H]
    u[1, :, :] = gw[:, H:R]
    w_u = push_core(u.at[o], c_in)
    w_u()
    u[c, :, :] = u[c] + c_in[...]
    z_in[z, :, :] = u[c, pl.ds(pl.multiple_of(z * zc, zc), zc), :]
    w_z3 = push_group(nz, zdev, lambda d: u.at[c, pl.ds(pl.multiple_of(zto(d) * zc, zc), zc)],
                      z_in.at[z], z_in.at[pl.ds(0, nz - 1)])
    w_z()
    w_q = chain_q(0)
    w_z3()
    tile = ma.at[c, pl.ds(pl.multiple_of(z * zc, zc), zc)]
    tile[...] = jnp.sum(z_in[...], axis=0)
    w_z4 = push_group(nz, zdev, lambda d: tile, tile, ma.at[c, pl.ds(0, yc - zc)])
    w_q()
    w_b = chain_back(0)
    w_b()
    h1 = chain_gram(0) * gram_c
    one = eye()
    inv = inverse_steps(inverse_start(h1, jnp.sum(h1 * one)), STEPS)
    x1 = inverse_end(inv)

    w_c()
    zero = jnp.zeros((1, R), f32)
    pad = [jnp.zeros((1, H), f32)] * (8 - nk)
    seg, half = lax.div(k, 2), lax.rem(k, 2)
    coef, totals, cols = [], [], []
    for kk in range(nk):
        grand = add([jnp.sum(chain_stat(0, ee * nk + kk, 1 + i), axis=1, keepdims=True)
                     for ee in range(ne) for i in range(ri // R)])
        coef.append(add([chain_stat(0, ee * nk + kk, 0) for ee in range(ne)]) * ws[kk:kk + 1] / grand)
        totals.append(xs[0, half, e * nk + kk, pl.ds(gs + 2 + seg, 1), :])
        cols.append(add([cq[ee * nk + kk] for ee in range(ne)]) / grand)
    coef = jnp.concatenate(coef + [zero] * (8 - nk), axis=0)
    totals = jnp.concatenate(totals + pad, axis=0)
    week = lax.broadcasted_iota(jnp.int32, (8, 1), 0)
    for kk in range(nk):
        only = (week == kk).astype(f32)
        res[:, kk * rj:(kk + 1) * rj] = fa[kk] - dot(totals * only, cols[kk] * only, 0, 0)
    fix = dot(totals, coef, 0, 0)

    w_z4()
    w_m = push_core(ma.at[c], ma.at[c])
    w_m()
    raw_a = dot(jnp.concatenate([ma[0], ma[1]], axis=1) - fix, x1)

    p0, p1, d = pack(dot(raw_a, raw_a, 0, 0))
    pk[0, :, :] = p0
    pk[1, :, :] = p1
    for i in range(nq):
        gx[i, 0:gs, :] = pk[c, i * gs:(i + 1) * gs, :]
        gx[i, gs:gs + 1, :] = d
    gi[q, :, :] = gx[q]
    w_gi = push_group(nq, qdev, lambda d: gx.at[qto(d)], gi.at[q], gi.at[pl.ds(0, nq - 1)])

    t = dot(res[...], raw_a, 0, 0)
    tw = add([t[i * rj:(i + 1) * rj] * ws[i:i + 1] for i in range(nk)])
    for i in range(nq):
        mos[i, :, :] = tw[i * jc:(i + 1) * jc]
    mi[q, :, :] = mos[q]
    w_mi = push_group(nq, qdev, lambda d: mos.at[qto(d)], mi.at[q], mi.at[pl.ds(0, nq - 1)])
    raw[0, k, :, :] = raw_a[:, 0:H]
    raw[1, k, :, :] = raw_a[:, H:R]

    w_gi()
    gsum = jnp.sum(gi[...], axis=0)
    mine = gag.at[c, pl.ds(pl.multiple_of(q * gs, gs), gs)]
    mine[...] = gsum[0:gs]
    w_ga = push_group(nq, qdev, lambda d: mine, mine, gag.at[c, pl.ds(0, H - gs)])
    w_mi()
    mo[q, :, :] = jnp.sum(mi[...], axis=0)
    w_mo = push_group(nq, qdev, lambda d: mo.at[q], mo.at[q], mo.at[pl.ds(0, nq - 1)])
    w_ga()
    w_gc = push_core(gag.at[c], gag.at[c])
    w_raw = push_group(nk, ydev, lambda d: raw.at[c, k], raw.at[c, k], raw.at[c, pl.ds(0, nk - 1)])
    w_gc()
    gram_a = unpack(gag[0], gag[1], gsum[gs:gs + 1])

    def unscale(gram, count):
        d = gram * one
        inv_row = 1.0 / jnp.sqrt(jnp.sum(d, axis=0, keepdims=True) / count + eps)
        inv_col = 1.0 / jnp.sqrt(jnp.sum(d, axis=1, keepdims=True) / count + eps)
        return inv_row, gram * inv_row * inv_col

    sa, gram_a = unscale(gram_a, ri * ne)
    h2 = gram_a * gram_c
    x2 = inverse_end(inverse_steps(inverse_start(h2, jnp.sum(h2 * one)), STEPS))
    w_mo()
    raw_b = dot(mo[...].reshape(rj, R) * sa, x2)

    chain_fill(1, dot(raw_b, raw_b, 0, 0),
               [jnp.sum(t[i * rj:(i + 1) * rj] * raw_b, axis=0, keepdims=True) for i in range(nk)])
    w_cs = chain_core(1)
    w_cs()
    w_z = chain_z(1)
    w_raw()
    w_rc = push_core(raw.at[c], raw.at[c])
    w_rc()
    a_out[:, 0:H] = raw[0].reshape(ri, H) * sa[:, 0:H]
    a_out[:, H:R] = raw[1].reshape(ri, H) * sa[:, H:R]
    w_z()
    w_q = chain_q(1)
    w_q()
    w_b = chain_back(1)
    w_b()
    sb, gram_b2 = unscale(chain_gram(1), rj * nz * 2)
    b_out[...] = raw_b * sb
    h3 = gram_a * gram_b2
    x3 = inverse_end(inverse_steps(inverse_start(h3, jnp.sum(h3 * one)), STEPS))
    scale = sa * sb
    m_c = jnp.concatenate([add([chain_stat(1, qq, kk) for qq in range(nq)]) * scale for kk in range(nk)] + [zero] * (8 - nk), axis=0)
    raw_c = dot(m_c, x3)
    sc = jnp.sqrt(jnp.sum(raw_c * raw_c, axis=0, keepdims=True) / nk + eps)
    c_out[...] = jnp.sum(raw_c * (week == k).astype(f32), axis=0, keepdims=True) / sc

    for fin in pending:
        fin()
    assert used[0] == NSEM


NSEM = 22


def per_device(ne, nz, nk, flows, importer_factor, week_factor):
    ri, rj = flows.shape[1], flows.shape[2]
    nq = ne * nk
    gs = H // nq
    yc = ri // nk
    vm = functools.partial(pltpu.VMEM, dtype=f32)
    return pl.pallas_call(
        functools.partial(kernel, ne, nz, nk),
        out_shape=(
            jax.ShapeDtypeStruct((ri, R), f32),
            jax.ShapeDtypeStruct((rj, R), f32),
            jax.ShapeDtypeStruct((1, R), f32),
        ),
        in_specs=[pl.BlockSpec(memory_space=pl.ANY)] * 3,
        out_specs=[pl.BlockSpec(memory_space=pltpu.VMEM)] * 3,
        scratch_shapes=[
            vm((ri, rj)),
            vm((rj, R)),
            vm((1, R)),
            vm((nk, yc, rj)),
            vm((2, yc, H)),
            vm((yc, H)),
            vm((nz, yc // nz, H)),
            vm((2, yc, H)),
            vm((nq, 1, rj)),
            vm((nk, 1, R)),
            vm((2, H, H)),
            vm((2, 2, gs + STATS, H)),
            vm((2, gs + STATS, H)),
            vm((2, nz, gs + STATS, H)),
            vm((2, 2, nq, gs + STATS, H)),
            vm((nq, gs + 1, H)),
            vm((nq, gs + 1, H)),
            vm((2, H, H)),
            vm((nq, rj // nq, R)),
            vm((nq, rj // nq, R)),
            vm((nq, rj // nq, R)),
            vm((yc, nk * rj)),
            vm((2, nk, yc, H)),
            pltpu.SemaphoreType.DMA((NSEM,)),
            pltpu.SemaphoreType.DMA((NSEM,)),
            pltpu.SemaphoreType.DMA((3,)),
        ],
        compiler_params=pltpu.CompilerParams(
            collective_id=0, has_side_effects=True, vmem_limit_bytes=60 * 1024 * 1024
        ),
    )(flows, importer_factor, week_factor)


def solution(mesh):
    in_specs = (P("wk", "exp", "imp"), P("imp", None), P("wk", None))
    out_specs = (P("exp", None), P("imp", None), P("wk", None))
    fn = functools.partial(per_device, mesh.shape["exp"], mesh.shape["imp"] // 2, mesh.shape["wk"])
    return jax.shard_map(fn, mesh=mesh, in_specs=in_specs, out_specs=out_specs, check_vma=False)
```

time: 108 us -> 86.4 us (0.80)
  Pallas kernels: 103 us -> 82.5 us
  local copies, waits for them, and re-layouts: 4.54 us -> 3.13 us
    pallas_call x1, Pallas kernels: 103 us -> 82.5 us  [per_device(): pl.pallas_call(functools.partial(kernel, ne, nz, nk), out_shape=(jax.Shap...]
    unnamed x9 -> x7, local copies, waits for them, and re-layouts: 4.54 us -> 3.13 us
where the time goes in v2:
time: 86.4 us; the launch traced here: 86.3 us
  Pallas kernels  82.5 us (95%)
  local copies, waits for them, and re-layouts  3.13 us (4%)
    pallas_call x1, Pallas kernels, per_device(): pl.pallas_call(functools.partial(kernel, ne, nz, nk), out_shape=(jax.Shap...  82.5 us
    unnamed x7, local copies, waits for them, and re-layouts  3.13 us

profile of v2, /device:TPU:1, one launch (start us, length us, event | category | flops | bytes accessed | tf_op | source)
XLA Modules:
  0.0 86.3 jit_solution(1725767052745680528)
XLA Ops:
  0.6 82.5 %shard_map.58 = (f32[512,256]{1,0:T(8,128)}, f32[128,256]{1,0:T(8,128)}, f32[1,256]{1,0:T(1,128)}) custom-call(f32[1,512,128]{2,1,0:T(8,128)} %f_hbm.1, f32[128,256]{1,0:T(8,128)} %b_hbm.1, f32[1,256]{1,0:T(1,128)} %w_hbm.1), custom_call_target="tpu_custom_call" | custom-call | tf_op jit(solution)/shard_map/pallas_call | solution.py:380
  83.1 0.0 copy-start
  83.1 1.9 %copy.9 = f32[512,256]{1,0:T(8,128)} copy(f32[512,256]{1,0:T(8,128)} %get-tuple-element.6) | data formatting | bytes 1048576
  85.0 0.0 copy-done
  85.0 0.0 copy-start.1
  85.1 0.7 copy.10
  85.7 0.0 copy-done.1
  85.7 0.6 copy.11
Async XLA Ops:
  83.1 1.9 %copy-start = (f32[128,256]{1,0:T(8,128)S(1)}, f32[128,256]{1,0:T(8,128)}, u32[]{:S(2)}) copy-start(f32[128,256]{1,0:T(8,128)} %get-tuple-element.7) | copy-start | bytes 393220
  85.0 0.7 copy-start.1

commit v3 on v2

--- a/solution.py
+++ b/solution.py
@@ -39,38 +39,23 @@
     return (lax.broadcasted_iota(jnp.int32, (R, R), 0) == lax.broadcasted_iota(jnp.int32, (R, R), 1)).astype(f32)
 
 
-def inverse_start(h, diag_sum):
-    lam = ridge * diag_sum / R
+def inverse(h):
     one = eye()
+    lam = ridge * jnp.sum(h * one) / R
     v = h + lam * one
     top = 1.0 + R / ridge
     alpha = 2.0 / (lam * (1.0 + top))
     delta = (top - 1.0) / (top + 1.0)
     e = one - alpha * v
-    x = None
-    return [v, e, x, alpha, delta, one]
-
-
-def inverse_steps(state, n):
-    v, e, x, alpha, delta, one = state
-    for _ in range(n):
+    for step in range(STEPS):
         c = 2.0 / (2.0 - delta * delta)
         delta = delta * delta / (2.0 - delta * delta)
         se = split(e)
-        if x is None:
-            x = (c * alpha) * (one + e)
-        else:
-            x = c * (x + dot3(split(x), se))
-        e = c * dot3(se, se) + (1.0 - c) * one
-    return [v, e, x, alpha, delta, one]
-
-
-def inverse_end(state):
-    v, e, x, alpha, delta, one = state
-    for _ in range(2):
-        r = one - dot(v, x)
-        x = x + dot3(split(x), split(r))
-    return x
+        x = (c * alpha) * (one + e) if step == 0 else c * (x + dot3(split(x), se))
+        if step < STEPS - 1:
+            e = c * dot3(se, se) + (1.0 - c) * one
+    r = one - dot(v, x)
+    return x + dot3(split(x), split(r))
 
 
 def triangle():
@@ -94,9 +79,9 @@
         [jnp.concatenate([g00, p1], axis=1), jnp.concatenate([p1.T, g11], axis=1)], axis=0)
 
 
-def kernel(ne, nz, nk, f_hbm, b_hbm, w_hbm, a_out, b_out, c_out,
+def kernel(ne, nz, nk, f_hbm, b_hbm, w_hbm, a_hbm, b_out_hbm, c_hbm,
            f_ref, b_ref, w_ref, fa, u, c_in, z_in, ma, cq, wx,
-           pk, cs, ci, zi, xs, gi, gx, gag, mi, mo, mos, res, raw,
+           pk, cs, ci, zi, xs, gi, gx, gag, mi, mo, mos, res, raw, a_out, b_out, c_out,
            ssem, rsem, lsem):
     e = lax.axis_index("exp")
     p = lax.axis_index("imp")
@@ -119,6 +104,8 @@
              pltpu.make_async_copy(w_hbm, w_ref, lsem.at[2])]
     for cp in loads:
         cp.start()
+    stores = [pltpu.make_async_copy(src, dst, lsem.at[3 + i])
+              for i, (src, dst) in enumerate([(a_out, a_hbm), (b_out, b_out_hbm), (c_out, c_hbm)])]
 
     def take():
         used[0] += 1
@@ -137,14 +124,14 @@
         pending.append(cp.wait_send)
         return cp.wait_recv
 
-    def push_group(n, dev, src, dst, every):
+    def push_group(n, dev, src, dst, every, first=1):
         s = take()
 
         def go(d, carry):
             remote(src(d), dst, s, dev(d)).start()
             return carry
 
-        lax.fori_loop(1, n, go, 0)
+        lax.fori_loop(first, n, go, 0)
         cp = remote(every, every, s, dev(1))
         pending.append(cp.wait_send)
         return cp.wait_recv
@@ -167,9 +154,10 @@
     def qdev(d):
         return {"exp": lax.div(qto(d), nk), "wk": lax.rem(qto(d), nk)}
 
+    def odev(d):
+        return {"exp": lax.div(qto(d), nk), "wk": lax.rem(qto(d), nk), "imp": z * 2 + o}
+
     barrier = pltpu.get_barrier_semaphore()
-    pl.semaphore_signal(barrier, inc=1, device_id=core_dev, device_id_type=MESH)
-
     def greet_z(d, carry):
         pl.semaphore_signal(barrier, inc=1, device_id=zdev(d), device_id_type=MESH)
         return carry
@@ -179,7 +167,12 @@
         return carry
 
     lax.fori_loop(1, nz, greet_z, 0)
+    def greet_o(d, carry):
+        pl.semaphore_signal(barrier, inc=1, device_id=odev(d), device_id_type=MESH)
+        return carry
+
     lax.fori_loop(1, nq, greet_q, 0)
+    lax.fori_loop(0, nq, greet_o, 0)
 
     def chain_fill(n, gram, stats):
         p0, p1, d = pack(gram)
@@ -202,10 +195,9 @@
 
     def chain_q(n):
         xs[n, c, q, :, :] = jnp.sum(zi[n], axis=0)
-        return push_group(nq, qdev, lambda d: xs.at[n, c, q], xs.at[n, c, q], xs.at[n, c, pl.ds(0, nq - 1)])
-
-    def chain_back(n):
-        return push_core(xs.at[n, c], xs.at[n, c])
+        mine = xs.at[n, c, q]
+        return (push_group(nq, qdev, lambda d: mine, mine, xs.at[n, c, pl.ds(0, nq - 1)]),
+                push_group(nq, odev, lambda d: mine, mine, xs.at[n, c], 0))
 
     def chain_gram(n):
         return unpack(xs[n, 0, :, 0:gs, :].reshape(H, H), xs[n, 1, :, 0:gs, :].reshape(H, H), xs[n, 0, 0, gs:gs + 1, :])
@@ -233,7 +225,7 @@
     chain_fill(0, dot(b, b, 0, 0), [v] + [rowp[0:1, i * R:(i + 1) * R] for i in range(ri // R)])
     fa[k, :, :] = f_ref[pl.ds(pl.multiple_of(k * yc, yc), yc), :]
 
-    pl.semaphore_wait(barrier, 1 + (nz - 1) + (nq - 1))
+    pl.semaphore_wait(barrier, (nz - 1) + (nq - 1) + nq)
 
     w_f = push_group(nk, ydev, lambda d: f_ref.at[pl.ds(pl.multiple_of(yto(d) * yc, yc), yc)], fa.at[k], fa.at[pl.ds(0, nk - 1)])
     w_cs = chain_core(0)
@@ -257,18 +249,16 @@
     w_z3 = push_group(nz, zdev, lambda d: u.at[c, pl.ds(pl.multiple_of(zto(d) * zc, zc), zc)],
                       z_in.at[z], z_in.at[pl.ds(0, nz - 1)])
     w_z()
-    w_q = chain_q(0)
+    w_q, w_b = chain_q(0)
     w_z3()
     tile = ma.at[c, pl.ds(pl.multiple_of(z * zc, zc), zc)]
     tile[...] = jnp.sum(z_in[...], axis=0)
     w_z4 = push_group(nz, zdev, lambda d: tile, tile, ma.at[c, pl.ds(0, yc - zc)])
     w_q()
-    w_b = chain_back(0)
     w_b()
     h1 = chain_gram(0) * gram_c
     one = eye()
-    inv = inverse_steps(inverse_start(h1, jnp.sum(h1 * one)), STEPS)
-    x1 = inverse_end(inv)
+    x1 = inverse(h1)
 
     w_c()
     zero = jnp.zeros((1, R), f32)
@@ -284,9 +274,6 @@
     coef = jnp.concatenate(coef + [zero] * (8 - nk), axis=0)
     totals = jnp.concatenate(totals + pad, axis=0)
     week = lax.broadcasted_iota(jnp.int32, (8, 1), 0)
-    for kk in range(nk):
-        only = (week == kk).astype(f32)
-        res[:, kk * rj:(kk + 1) * rj] = fa[kk] - dot(totals * only, cols[kk] * only, 0, 0)
     fix = dot(totals, coef, 0, 0)
 
     w_z4()
@@ -303,6 +290,9 @@
     gi[q, :, :] = gx[q]
     w_gi = push_group(nq, qdev, lambda d: gx.at[qto(d)], gi.at[q], gi.at[pl.ds(0, nq - 1)])
 
+    for kk in range(nk):
+        only = (week == kk).astype(f32)
+        res[:, kk * rj:(kk + 1) * rj] = fa[kk] - dot(totals * only, cols[kk] * only, 0, 0)
     t = dot(res[...], raw_a, 0, 0)
     tw = add([t[i * rj:(i + 1) * rj] * ws[i:i + 1] for i in range(nk)])
     for i in range(nq):
@@ -317,11 +307,11 @@
     mine = gag.at[c, pl.ds(pl.multiple_of(q * gs, gs), gs)]
     mine[...] = gsum[0:gs]
     w_ga = push_group(nq, qdev, lambda d: mine, mine, gag.at[c, pl.ds(0, H - gs)])
+    w_gc = push_group(nq, odev, lambda d: mine, mine, gag.at[c], 0)
     w_mi()
     mo[q, :, :] = jnp.sum(mi[...], axis=0)
     w_mo = push_group(nq, qdev, lambda d: mo.at[q], mo.at[q], mo.at[pl.ds(0, nq - 1)])
     w_ga()
-    w_gc = push_core(gag.at[c], gag.at[c])
     w_raw = push_group(nk, ydev, lambda d: raw.at[c, k], raw.at[c, k], raw.at[c, pl.ds(0, nk - 1)])
     w_gc()
     gram_a = unpack(gag[0], gag[1], gsum[gs:gs + 1])
@@ -334,7 +324,7 @@
 
     sa, gram_a = unscale(gram_a, ri * ne)
     h2 = gram_a * gram_c
-    x2 = inverse_end(inverse_steps(inverse_start(h2, jnp.sum(h2 * one)), STEPS))
+    x2 = inverse(h2)
     w_mo()
     raw_b = dot(mo[...].reshape(rj, R) * sa, x2)
 
@@ -348,27 +338,44 @@
     w_rc()
     a_out[:, 0:H] = raw[0].reshape(ri, H) * sa[:, 0:H]
     a_out[:, H:R] = raw[1].reshape(ri, H) * sa[:, H:R]
+    stores[0].start()
     w_z()
-    w_q = chain_q(1)
+    w_q, w_b = chain_q(1)
     w_q()
-    w_b = chain_back(1)
     w_b()
     sb, gram_b2 = unscale(chain_gram(1), rj * nz * 2)
     b_out[...] = raw_b * sb
+    stores[1].start()
     h3 = gram_a * gram_b2
-    x3 = inverse_end(inverse_steps(inverse_start(h3, jnp.sum(h3 * one)), STEPS))
+    x3 = inverse(h3)
     scale = sa * sb
     m_c = jnp.concatenate([add([chain_stat(1, qq, kk) for qq in range(nq)]) * scale for kk in range(nk)] + [zero] * (8 - nk), axis=0)
     raw_c = dot(m_c, x3)
     sc = jnp.sqrt(jnp.sum(raw_c * raw_c, axis=0, keepdims=True) / nk + eps)
     c_out[...] = jnp.sum(raw_c * (week == k).astype(f32), axis=0, keepdims=True) / sc
+    stores[2].start()
 
     for fin in pending:
         fin()
+    for cp in stores:
+        cp.wait()
     assert used[0] == NSEM
 
 
 NSEM = 22
+PARTS = 4
+
+
+def hand_over(a_in, b_in, c_in, a_out, b_out, c_out, sems):
+    rows = a_in.shape[0] // PARTS
+    copies = [pltpu.make_async_copy(a_in.at[pl.ds(i * rows, rows)], a_out.at[pl.ds(i * rows, rows)], sems.at[i])
+              for i in range(PARTS)]
+    copies.append(pltpu.make_async_copy(b_in, b_out, sems.at[PARTS]))
+    copies.append(pltpu.make_async_copy(c_in, c_out, sems.at[PARTS + 1]))
+    for cp in copies:
+        cp.start()
+    for cp in copies:
+        cp.wait()
 
 
 def per_device(ne, nz, nk, flows, importer_factor, week_factor):
@@ -377,15 +384,16 @@
     gs = H // nq
     yc = ri // nk
     vm = functools.partial(pltpu.VMEM, dtype=f32)
-    return pl.pallas_call(
+    shapes = (
+        jax.ShapeDtypeStruct((ri, R), f32),
+        jax.ShapeDtypeStruct((rj, R), f32),
+        jax.ShapeDtypeStruct((1, R), f32),
+    )
+    outs = pl.pallas_call(
         functools.partial(kernel, ne, nz, nk),
-        out_shape=(
-            jax.ShapeDtypeStruct((ri, R), f32),
-            jax.ShapeDtypeStruct((rj, R), f32),
-            jax.ShapeDtypeStruct((1, R), f32),
-        ),
+        out_shape=shapes,
         in_specs=[pl.BlockSpec(memory_space=pl.ANY)] * 3,
-        out_specs=[pl.BlockSpec(memory_space=pltpu.VMEM)] * 3,
+        out_specs=[pl.BlockSpec(memory_space=pl.ANY)] * 3,
         scratch_shapes=[
             vm((ri, rj)),
             vm((rj, R)),
@@ -410,14 +418,24 @@
             vm((nq, rj // nq, R)),
             vm((yc, nk * rj)),
             vm((2, nk, yc, H)),
+            vm((ri, R)),
+            vm((rj, R)),
+            vm((1, R)),
             pltpu.SemaphoreType.DMA((NSEM,)),
             pltpu.SemaphoreType.DMA((NSEM,)),
-            pltpu.SemaphoreType.DMA((3,)),
+            pltpu.SemaphoreType.DMA((6,)),
         ],
         compiler_params=pltpu.CompilerParams(
             collective_id=0, has_side_effects=True, vmem_limit_bytes=60 * 1024 * 1024
         ),
     )(flows, importer_factor, week_factor)
+    return pl.pallas_call(
+        hand_over,
+        out_shape=shapes,
+        in_specs=[pl.BlockSpec(memory_space=pl.ANY)] * 3,
+        out_specs=[pl.BlockSpec(memory_space=pl.ANY)] * 3,
+        scratch_shapes=[pltpu.SemaphoreType.DMA((PARTS + 2,))],
+    )(*outs)
 
 
 def solution(mesh):

time: 86.4 us -> 102 us (1.18)
  Pallas kernels: 82.5 us -> 101 us
  local copies, waits for them, and re-layouts: 3.13 us -> 0 us
    pallas_call x1 -> x2, Pallas kernels: 82.5 us -> 101 us  [the longest x1 80.1 us: per_device(): pl.pallas_call(functools.partial(kernel, ne, nz, nk), out_shape=shapes, i...]
    unnamed x7 -> x0, local copies, waits for them, and re-layouts: 3.13 us -> none
where the time goes in v3:
time: 102 us
  Pallas kernels  101 us (99%)
    pallas_call x1, Pallas kernels, per_device(): pl.pallas_call(functools.partial(kernel, ne, nz, nk), out_shape=shapes, i...  80.1 us
    pallas_call x1, Pallas kernels, per_device(): pl.pallas_call(hand_over, out_shape=shapes, in_specs=[pl.BlockSpec(memory...  21 us

profile of v3, /device:TPU:1, one launch (start us, length us, event | category | flops | bytes accessed | tf_op | source)
XLA Modules:
  0.0 101.7 jit_solution(14420760872641327791)
XLA Ops:
  0.6 80.1 %shard_map.58 = (f32[512,256]{1,0:T(8,128)}, f32[128,256]{1,0:T(8,128)}, f32[1,256]{1,0:T(1,128)}) custom-call(f32[1,512,128]{2,1,0:T(8,128)} %f_hbm.1, f32[128,256]{1,0:T(8,128)} %b_hbm.1, f32[1,256]{1,0:T(1,128)} %w_hbm.1), custom_call_target="tpu_custom_call" | custom-call | tf_op jit(solution)/shard_map/pallas_call | solution.py:392
  80.7 21.0 %shard_map.59 = (f32[512,256]{1,0:T(8,128)}, f32[128,256]{1,0:T(8,128)}, f32[1,256]{1,0:T(1,128)}) custom-call(f32[512,256]{1,0:T(8,128)} %get-tuple-element.6.a_in, f32[128,256]{1,0:T(8,128)} %get-tuple-element.7.b_in, f32[1,256]{1,0:T(1,128)} %get-tuple-element.8.c_in), custom_call_target="tpu_custom_call" | custom-call | tf_op jit(solution)/shard_map/pallas_call | solution.py:432

commit v4 on v3

--- a/solution.py
+++ b/solution.py
@@ -366,15 +366,19 @@
 PARTS = 4
 
 
-def hand_over(a_in, b_in, c_in, a_out, b_out, c_out, sems):
+def hand_over(a_in, b_in, c_in, a_out, b_out, c_out, a, b, c, load, store):
     rows = a_in.shape[0] // PARTS
-    copies = [pltpu.make_async_copy(a_in.at[pl.ds(i * rows, rows)], a_out.at[pl.ds(i * rows, rows)], sems.at[i])
-              for i in range(PARTS)]
-    copies.append(pltpu.make_async_copy(b_in, b_out, sems.at[PARTS]))
-    copies.append(pltpu.make_async_copy(c_in, c_out, sems.at[PARTS + 1]))
-    for cp in copies:
+    steps = [(x_in.at[pl.ds(i * n, n)], x.at[pl.ds(i * n, n)], x_out.at[pl.ds(i * n, n)])
+             for x_in, x, x_out, n, parts in ((a_in, a, a_out, rows, PARTS), (b_in, b, b_out, b_in.shape[0], 1))
+             for i in range(parts)] + [(c_in, c, c_out)]
+    loads = [pltpu.make_async_copy(src, mid, load.at[i]) for i, (src, mid, dst) in enumerate(steps)]
+    stores = [pltpu.make_async_copy(mid, dst, store.at[i]) for i, (src, mid, dst) in enumerate(steps)]
+    for cp in loads:
         cp.start()
-    for cp in copies:
+    for first, then in zip(loads, stores):
+        first.wait()
+        then.start()
+    for cp in stores:
         cp.wait()
 
 
@@ -434,7 +438,7 @@
         out_shape=shapes,
         in_specs=[pl.BlockSpec(memory_space=pl.ANY)] * 3,
         out_specs=[pl.BlockSpec(memory_space=pl.ANY)] * 3,
-        scratch_shapes=[pltpu.SemaphoreType.DMA((PARTS + 2,))],
+        scratch_shapes=[vm((ri, R)), vm((rj, R)), vm((1, R))] + [pltpu.SemaphoreType.DMA((PARTS + 2,))] * 2,
     )(*outs)
 
 

time: 102 us -> 82.8 us (0.81)
  Pallas kernels: 101 us -> 82 us
    pallas_call x1, Pallas kernels: 21 us -> 1.93 us  [per_device(): pl.pallas_call(hand_over, out_shape=shapes, in_specs=[pl.BlockSpec(memory...]
where the time goes in v4:
time: 82.8 us; the launch traced here: 82.6 us
  Pallas kernels  82 us (99%)
    pallas_call x1, Pallas kernels, per_device(): pl.pallas_call(functools.partial(kernel, ne, nz, nk), out_shape=shapes, i...  80.1 us
    pallas_call x1, Pallas kernels, per_device(): pl.pallas_call(hand_over, out_shape=shapes, in_specs=[pl.BlockSpec(memory...  1.93 us

profile of v4, /device:TPU:1, one launch (start us, length us, event | category | flops | bytes accessed | tf_op | source)
XLA Modules:
  0.0 82.6 jit_solution(7266673676851043072)
XLA Ops:
  0.6 80.1 %shard_map.58 = (f32[512,256]{1,0:T(8,128)}, f32[128,256]{1,0:T(8,128)}, f32[1,256]{1,0:T(1,128)}) custom-call(f32[1,512,128]{2,1,0:T(8,128)} %f_hbm.1, f32[128,256]{1,0:T(8,128)} %b_hbm.1, f32[1,256]{1,0:T(1,128)} %w_hbm.1), custom_call_target="tpu_custom_call" | custom-call | tf_op jit(solution)/shard_map/pallas_call | solution.py:396
  80.7 1.9 %shard_map.59 = (f32[512,256]{1,0:T(8,128)}, f32[128,256]{1,0:T(8,128)}, f32[1,256]{1,0:T(1,128)}) custom-call(f32[512,256]{1,0:T(8,128)} %get-tuple-element.6.a_in, f32[128,256]{1,0:T(8,128)} %get-tuple-element.7.b_in, f32[1,256]{1,0:T(1,128)} %get-tuple-element.8.c_in), custom_call_target="tpu_custom_call" | custom-call | tf_op jit(solution)/shard_map/pallas_call | solution.py:436

commit v5 on v4

--- a/solution.py
+++ b/solution.py
@@ -39,7 +39,7 @@
     return (lax.broadcasted_iota(jnp.int32, (R, R), 0) == lax.broadcasted_iota(jnp.int32, (R, R), 1)).astype(f32)
 
 
-def inverse(h):
+def nearly(h):
     one = eye()
     lam = ridge * jnp.sum(h * one) / R
     v = h + lam * one
@@ -54,8 +54,19 @@
         x = (c * alpha) * (one + e) if step == 0 else c * (x + dot3(split(x), se))
         if step < STEPS - 1:
             e = c * dot3(se, se) + (1.0 - c) * one
-    r = one - dot(v, x)
-    return x + dot3(split(x), split(r))
+    return v, x
+
+
+def inverse(h):
+    v, x = nearly(h)
+    return x + dot3(split(x), split(eye() - dot(v, x)))
+
+
+def solve(m, h):
+    v, x = nearly(h)
+    x = split(x)
+    y = dot3(split(m), x)
+    return y + dot3(split(m - dot(y, v)), x)
 
 
 def triangle():
@@ -80,7 +91,7 @@
 
 
 def kernel(ne, nz, nk, f_hbm, b_hbm, w_hbm, a_hbm, b_out_hbm, c_hbm,
-           f_ref, b_ref, w_ref, fa, u, c_in, z_in, ma, cq, wx,
+           f_ref, b_ref, w_ref, fa, u, z_in, ma, cq, wx,
            pk, cs, ci, zi, xs, gi, gx, gag, mi, mo, mos, res, raw, a_out, b_out, c_out,
            ssem, rsem, lsem):
     e = lax.axis_index("exp")
@@ -127,21 +138,50 @@
     def push_group(n, dev, src, dst, every, first=1):
         s = take()
 
-        def go(d, carry):
+        def go(i, carry):
+            d = far(i, n)
             remote(src(d), dst, s, dev(d)).start()
             return carry
 
-        lax.fori_loop(first, n, go, 0)
+        lax.fori_loop(0, n - first, go, 0)
         cp = remote(every, every, s, dev(1))
         pending.append(cp.wait_send)
         return cp.wait_recv
 
+    def push_both(n, dev, dev_o, src, src_o, dst, every, every_o):
+        s, s_o = take(), take()
+
+        def go(i, carry):
+            d = far(i, n)
+            remote(src(d), dst, s, dev(d)).start()
+            remote(src_o(d), dst, s_o, dev_o(d)).start()
+            return carry
+
+        lax.fori_loop(0, n - 1, go, 0)
+        remote(src_o(0), dst, s_o, dev_o(0)).start()
+        cp = remote(every, every, s, dev(1))
+        cp_o = remote(every_o, every_o, s_o, dev_o(0))
+        pending.extend([cp.wait_send, cp_o.wait_send])
+
+        def wait():
+            cp.wait_recv()
+            cp_o.wait_recv()
+
+        return wait
+
+    def far(i, n):
+        h = lax.div(i + 1, 2)
+        return lax.rem(n // 2 + jnp.where(lax.rem(i, 2) == 1, h, -h), n)
+
     def zto(d):
         return lax.rem(z + d, nz)
 
     def zdev(d):
         return {"imp": zto(d) * 2 + c}
 
+    def zodev(d):
+        return {"imp": zto(d) * 2 + o}
+
     def yto(d):
         return lax.rem(k + d, nk)
 
@@ -158,21 +198,17 @@
         return {"exp": lax.div(qto(d), nk), "wk": lax.rem(qto(d), nk), "imp": z * 2 + o}
 
     barrier = pltpu.get_barrier_semaphore()
-    def greet_z(d, carry):
-        pl.semaphore_signal(barrier, inc=1, device_id=zdev(d), device_id_type=MESH)
-        return carry
-
-    def greet_q(d, carry):
-        pl.semaphore_signal(barrier, inc=1, device_id=qdev(d), device_id_type=MESH)
-        return carry
-
-    lax.fori_loop(1, nz, greet_z, 0)
-    def greet_o(d, carry):
-        pl.semaphore_signal(barrier, inc=1, device_id=odev(d), device_id_type=MESH)
-        return carry
-
-    lax.fori_loop(1, nq, greet_q, 0)
-    lax.fori_loop(0, nq, greet_o, 0)
+    def greet(n, first, dev):
+        def one_device(i, carry):
+            pl.semaphore_signal(barrier, inc=1, device_id=dev(far(i, n)), device_id_type=MESH)
+            return carry
+
+        lax.fori_loop(0, n - first, one_device, 0)
+
+    greet(nz, 1, zdev)
+    greet(nz, 0, zodev)
+    greet(nq, 1, qdev)
+    greet(nq, 1, odev)
 
     def chain_fill(n, gram, stats):
         p0, p1, d = pack(gram)
@@ -196,8 +232,7 @@
     def chain_q(n):
         xs[n, c, q, :, :] = jnp.sum(zi[n], axis=0)
         mine = xs.at[n, c, q]
-        return (push_group(nq, qdev, lambda d: mine, mine, xs.at[n, c, pl.ds(0, nq - 1)]),
-                push_group(nq, odev, lambda d: mine, mine, xs.at[n, c], 0))
+        return push_both(nq, qdev, odev, lambda d: mine, lambda d: mine, mine, xs.at[n, c, pl.ds(0, nq - 1)], xs.at[n, c])
 
     def chain_gram(n):
         return unpack(xs[n, 0, :, 0:gs, :].reshape(H, H), xs[n, 1, :, 0:gs, :].reshape(H, H), xs[n, 0, 0, gs:gs + 1, :])
@@ -225,7 +260,7 @@
     chain_fill(0, dot(b, b, 0, 0), [v] + [rowp[0:1, i * R:(i + 1) * R] for i in range(ri // R)])
     fa[k, :, :] = f_ref[pl.ds(pl.multiple_of(k * yc, yc), yc), :]
 
-    pl.semaphore_wait(barrier, (nz - 1) + (nq - 1) + nq)
+    pl.semaphore_wait(barrier, (nz - 1) + nz + 2 * (nq - 1))
 
     w_f = push_group(nk, ydev, lambda d: f_ref.at[pl.ds(pl.multiple_of(yto(d) * yc, yc), yc)], fa.at[k], fa.at[pl.ds(0, nk - 1)])
     w_cs = chain_core(0)
@@ -242,20 +277,19 @@
     gw = add([g[i * yc:(i + 1) * yc] * ws[i:i + 1] for i in range(nk)])
     u[0, :, :] = gw[:, 0:H]
     u[1, :, :] = gw[:, H:R]
-    w_u = push_core(u.at[o], c_in)
-    w_u()
-    u[c, :, :] = u[c] + c_in[...]
-    z_in[z, :, :] = u[c, pl.ds(pl.multiple_of(z * zc, zc), zc), :]
-    w_z3 = push_group(nz, zdev, lambda d: u.at[c, pl.ds(pl.multiple_of(zto(d) * zc, zc), zc)],
-                      z_in.at[z], z_in.at[pl.ds(0, nz - 1)])
+    def cut(h, zz):
+        return u.at[h, pl.ds(pl.multiple_of(zz * zc, zc), zc)]
+
+    z_in[p, :, :] = cut(c, z)[...]
+    w_z3 = push_both(nz, zdev, zodev, lambda d: cut(c, zto(d)), lambda d: cut(o, zto(d)), z_in.at[p],
+                     z_in.at[pl.ds(0, nz - 1)], z_in.at[pl.ds(0, nz)])
     w_z()
-    w_q, w_b = chain_q(0)
+    w_q = chain_q(0)
     w_z3()
     tile = ma.at[c, pl.ds(pl.multiple_of(z * zc, zc), zc)]
     tile[...] = jnp.sum(z_in[...], axis=0)
-    w_z4 = push_group(nz, zdev, lambda d: tile, tile, ma.at[c, pl.ds(0, yc - zc)])
+    w_z4 = push_both(nz, zdev, zodev, lambda d: tile, lambda d: tile, tile, ma.at[c, pl.ds(0, yc - zc)], ma.at[c])
     w_q()
-    w_b()
     h1 = chain_gram(0) * gram_c
     one = eye()
     x1 = inverse(h1)
@@ -277,8 +311,6 @@
     fix = dot(totals, coef, 0, 0)
 
     w_z4()
-    w_m = push_core(ma.at[c], ma.at[c])
-    w_m()
     raw_a = dot(jnp.concatenate([ma[0], ma[1]], axis=1) - fix, x1)
 
     p0, p1, d = pack(dot(raw_a, raw_a, 0, 0))
@@ -306,14 +338,12 @@
     gsum = jnp.sum(gi[...], axis=0)
     mine = gag.at[c, pl.ds(pl.multiple_of(q * gs, gs), gs)]
     mine[...] = gsum[0:gs]
-    w_ga = push_group(nq, qdev, lambda d: mine, mine, gag.at[c, pl.ds(0, H - gs)])
-    w_gc = push_group(nq, odev, lambda d: mine, mine, gag.at[c], 0)
+    w_ga = push_both(nq, qdev, odev, lambda d: mine, lambda d: mine, mine, gag.at[c, pl.ds(0, H - gs)], gag.at[c])
     w_mi()
     mo[q, :, :] = jnp.sum(mi[...], axis=0)
     w_mo = push_group(nq, qdev, lambda d: mo.at[q], mo.at[q], mo.at[pl.ds(0, nq - 1)])
     w_ga()
     w_raw = push_group(nk, ydev, lambda d: raw.at[c, k], raw.at[c, k], raw.at[c, pl.ds(0, nk - 1)])
-    w_gc()
     gram_a = unpack(gag[0], gag[1], gsum[gs:gs + 1])
 
     def unscale(gram, count):
@@ -324,9 +354,8 @@
 
     sa, gram_a = unscale(gram_a, ri * ne)
     h2 = gram_a * gram_c
-    x2 = inverse(h2)
     w_mo()
-    raw_b = dot(mo[...].reshape(rj, R) * sa, x2)
+    raw_b = solve(mo[...].reshape(rj, R) * sa, h2)
 
     chain_fill(1, dot(raw_b, raw_b, 0, 0),
                [jnp.sum(t[i * rj:(i + 1) * rj] * raw_b, axis=0, keepdims=True) for i in range(nk)])
@@ -340,17 +369,15 @@
     a_out[:, H:R] = raw[1].reshape(ri, H) * sa[:, H:R]
     stores[0].start()
     w_z()
-    w_q, w_b = chain_q(1)
+    w_q = chain_q(1)
     w_q()
-    w_b()
     sb, gram_b2 = unscale(chain_gram(1), rj * nz * 2)
     b_out[...] = raw_b * sb
     stores[1].start()
     h3 = gram_a * gram_b2
-    x3 = inverse(h3)
     scale = sa * sb
     m_c = jnp.concatenate([add([chain_stat(1, qq, kk) for qq in range(nq)]) * scale for kk in range(nk)] + [zero] * (8 - nk), axis=0)
-    raw_c = dot(m_c, x3)
+    raw_c = solve(m_c, h3)
     sc = jnp.sqrt(jnp.sum(raw_c * raw_c, axis=0, keepdims=True) / nk + eps)
     c_out[...] = jnp.sum(raw_c * (week == k).astype(f32), axis=0, keepdims=True) / sc
     stores[2].start()
@@ -404,8 +431,7 @@
             vm((1, R)),
             vm((nk, yc, rj)),
             vm((2, yc, H)),
-            vm((yc, H)),
-            vm((nz, yc // nz, H)),
+            vm((2 * nz, yc // nz, H)),
             vm((2, yc, H)),
             vm((nq, 1, rj)),
             vm((nk, 1, R)),

time: 82.8 us -> 81.2 us (0.981)
  Pallas kernels: 82 us -> 80.4 us
    pallas_call x1, Pallas kernels: 80.1 us -> 78.5 us  [per_device(): pl.pallas_call(functools.partial(kernel, ne, nz, nk), out_shape=shapes, i...]
where the time goes in v5:
time: 81.2 us; the launch traced here: 81.1 us
  Pallas kernels  80.4 us (99%)
    pallas_call x1, Pallas kernels, per_device(): pl.pallas_call(functools.partial(kernel, ne, nz, nk), out_shape=shapes, i...  78.5 us
    pallas_call x1, Pallas kernels, per_device(): pl.pallas_call(hand_over, out_shape=shapes, in_specs=[pl.BlockSpec(memory...  1.93 us

profile of v5, /device:TPU:1, one launch (start us, length us, event | category | flops | bytes accessed | tf_op | source)
XLA Modules:
  0.0 81.1 jit_solution(12957133088576664441)
XLA Ops:
  0.6 78.5 %shard_map.58 = (f32[512,256]{1,0:T(8,128)}, f32[128,256]{1,0:T(8,128)}, f32[1,256]{1,0:T(1,128)}) custom-call(f32[1,512,128]{2,1,0:T(8,128)} %f_hbm.1, f32[128,256]{1,0:T(8,128)} %b_hbm.1, f32[1,256]{1,0:T(1,128)} %w_hbm.1), custom_call_target="tpu_custom_call" | custom-call | tf_op jit(solution)/shard_map/pallas_call | solution.py:423
  79.1 1.9 %shard_map.59 = (f32[512,256]{1,0:T(8,128)}, f32[128,256]{1,0:T(8,128)}, f32[1,256]{1,0:T(1,128)}) custom-call(f32[512,256]{1,0:T(8,128)} %get-tuple-element.6.a_in, f32[128,256]{1,0:T(8,128)} %get-tuple-element.7.b_in, f32[1,256]{1,0:T(1,128)} %get-tuple-element.8.c_in), custom_call_target="tpu_custom_call" | custom-call | tf_op jit(solution)/shard_map/pallas_call | solution.py:462

commit v6 on v5

--- a/solution.py
+++ b/solution.py
@@ -91,7 +91,7 @@
 
 
 def kernel(ne, nz, nk, f_hbm, b_hbm, w_hbm, a_hbm, b_out_hbm, c_hbm,
-           f_ref, b_ref, w_ref, fa, u, z_in, ma, cq, wx,
+           f_ref, b_ref, w_ref, fa, u, c_in, z_in, ma, cq, wx,
            pk, cs, ci, zi, xs, gi, gx, gag, mi, mo, mos, res, raw, a_out, b_out, c_out,
            ssem, rsem, lsem):
     e = lax.axis_index("exp")
@@ -206,9 +206,8 @@
         lax.fori_loop(0, n - first, one_device, 0)
 
     greet(nz, 1, zdev)
-    greet(nz, 0, zodev)
     greet(nq, 1, qdev)
-    greet(nq, 1, odev)
+    greet(nq, 0, odev)
 
     def chain_fill(n, gram, stats):
         p0, p1, d = pack(gram)
@@ -260,7 +259,7 @@
     chain_fill(0, dot(b, b, 0, 0), [v] + [rowp[0:1, i * R:(i + 1) * R] for i in range(ri // R)])
     fa[k, :, :] = f_ref[pl.ds(pl.multiple_of(k * yc, yc), yc), :]
 
-    pl.semaphore_wait(barrier, (nz - 1) + nz + 2 * (nq - 1))
+    pl.semaphore_wait(barrier, (nz - 1) + (nq - 1) + nq)
 
     w_f = push_group(nk, ydev, lambda d: f_ref.at[pl.ds(pl.multiple_of(yto(d) * yc, yc), yc)], fa.at[k], fa.at[pl.ds(0, nk - 1)])
     w_cs = chain_core(0)
@@ -280,15 +279,17 @@
     def cut(h, zz):
         return u.at[h, pl.ds(pl.multiple_of(zz * zc, zc), zc)]
 
-    z_in[p, :, :] = cut(c, z)[...]
-    w_z3 = push_both(nz, zdev, zodev, lambda d: cut(c, zto(d)), lambda d: cut(o, zto(d)), z_in.at[p],
-                     z_in.at[pl.ds(0, nz - 1)], z_in.at[pl.ds(0, nz)])
+    w_u = push_core(u.at[o], c_in)
+    w_u()
+    u[c, :, :] = u[c] + c_in[...]
+    z_in[z, :, :] = cut(c, z)[...]
+    w_z3 = push_group(nz, zdev, lambda d: cut(c, zto(d)), z_in.at[z], z_in.at[pl.ds(0, nz - 1)])
     w_z()
     w_q = chain_q(0)
     w_z3()
     tile = ma.at[c, pl.ds(pl.multiple_of(z * zc, zc), zc)]
     tile[...] = jnp.sum(z_in[...], axis=0)
-    w_z4 = push_both(nz, zdev, zodev, lambda d: tile, lambda d: tile, tile, ma.at[c, pl.ds(0, yc - zc)], ma.at[c])
+    w_z4 = push_group(nz, zdev, lambda d: tile, tile, ma.at[c, pl.ds(0, yc - zc)])
     w_q()
     h1 = chain_gram(0) * gram_c
     one = eye()
@@ -311,6 +312,8 @@
     fix = dot(totals, coef, 0, 0)
 
     w_z4()
+    w_m = push_core(ma.at[c], ma.at[c])
+    w_m()
     raw_a = dot(jnp.concatenate([ma[0], ma[1]], axis=1) - fix, x1)
 
     p0, p1, d = pack(dot(raw_a, raw_a, 0, 0))
@@ -431,7 +434,8 @@
             vm((1, R)),
             vm((nk, yc, rj)),
             vm((2, yc, H)),
-            vm((2 * nz, yc // nz, H)),
+            vm((yc, H)),
+            vm((nz, yc // nz, H)),
             vm((2, yc, H)),
             vm((nq, 1, rj)),
             vm((nk, 1, R)),

time: 81.2 us -> 78.1 us (0.962)
  Pallas kernels: 80.4 us -> 77.3 us
    pallas_call x1, Pallas kernels: 78.5 us -> 75.4 us  [per_device(): pl.pallas_call(functools.partial(kernel, ne, nz, nk), out_shape=shapes, i...]
where the time goes in v6:
time: 78.1 us; the launch traced here: 78 us
  Pallas kernels  77.3 us (99%)
    pallas_call x1, Pallas kernels, per_device(): pl.pallas_call(functools.partial(kernel, ne, nz, nk), out_shape=shapes, i...  75.4 us
    pallas_call x1, Pallas kernels, per_device(): pl.pallas_call(hand_over, out_shape=shapes, in_specs=[pl.BlockSpec(memory...  1.93 us

profile of v6, /device:TPU:1, one launch (start us, length us, event | category | flops | bytes accessed | tf_op | source)
XLA Modules:
  0.0 78.0 jit_solution(1616445740617898533)
XLA Ops:
  0.6 75.4 %shard_map.58 = (f32[512,256]{1,0:T(8,128)}, f32[128,256]{1,0:T(8,128)}, f32[1,256]{1,0:T(1,128)}) custom-call(f32[1,512,128]{2,1,0:T(8,128)} %f_hbm.1, f32[128,256]{1,0:T(8,128)} %b_hbm.1, f32[1,256]{1,0:T(1,128)} %w_hbm.1), custom_call_target="tpu_custom_call" | custom-call | tf_op jit(solution)/shard_map/pallas_call | solution.py:426
  76.0 1.9 %shard_map.59 = (f32[512,256]{1,0:T(8,128)}, f32[128,256]{1,0:T(8,128)}, f32[1,256]{1,0:T(1,128)}) custom-call(f32[512,256]{1,0:T(8,128)} %get-tuple-element.6.a_in, f32[128,256]{1,0:T(8,128)} %get-tuple-element.7.b_in, f32[1,256]{1,0:T(1,128)} %get-tuple-element.8.c_in), custom_call_target="tpu_custom_call" | custom-call | tf_op jit(solution)/shard_map/pallas_call | solution.py:466

commit v7 on v6

--- a/solution.py
+++ b/solution.py
@@ -91,7 +91,7 @@
 
 
 def kernel(ne, nz, nk, f_hbm, b_hbm, w_hbm, a_hbm, b_out_hbm, c_hbm,
-           f_ref, b_ref, w_ref, fa, u, c_in, z_in, ma, cq, wx,
+           f_ref, b_ref, w_ref, fa, u, c_in, zb, vs, z_in, ma, cq, wx,
            pk, cs, ci, zi, xs, gi, gx, gag, mi, mo, mos, res, raw, a_out, b_out, c_out,
            ssem, rsem, lsem):
     e = lax.axis_index("exp")
@@ -206,8 +206,9 @@
         lax.fori_loop(0, n - first, one_device, 0)
 
     greet(nz, 1, zdev)
+    greet(nz, 0, zodev)
     greet(nq, 1, qdev)
-    greet(nq, 0, odev)
+    greet(nq, 1, odev)
 
     def chain_fill(n, gram, stats):
         p0, p1, d = pack(gram)
@@ -230,6 +231,8 @@
 
     def chain_q(n):
         xs[n, c, q, :, :] = jnp.sum(zi[n], axis=0)
+        if n == 0:
+            xs[n, c, q, gs + 1:gs + 2, :] = xs[n, c, q, gs + 1:gs + 2, :] + vs[c]
         mine = xs.at[n, c, q]
         return push_both(nq, qdev, odev, lambda d: mine, lambda d: mine, mine, xs.at[n, c, pl.ds(0, nq - 1)], xs.at[n, c])
 
@@ -250,19 +253,24 @@
     f = f_ref[...]
     b = b_ref[...]
     w = w_ref[...]
-    shifted = b - 0.5
+    own = jnp.sum(b, axis=0, keepdims=True) / rj
+    shifted = b - own
     wx[k, :, :] = w
     rowp = dot(jnp.ones((8, rj), f32), f, 1, 1)
     colp = jnp.sum(f, axis=0, keepdims=True)
     cq[q, :, :] = colp
+    zb[p, 0:1, :] = own
+    zb[p, 1:2, :] = jnp.broadcast_to(jnp.sum(colp, axis=1, keepdims=True), (1, R))
     v = dot(jnp.broadcast_to(colp, (8, rj)), shifted)[0:1]
     chain_fill(0, dot(b, b, 0, 0), [v] + [rowp[0:1, i * R:(i + 1) * R] for i in range(ri // R)])
     fa[k, :, :] = f_ref[pl.ds(pl.multiple_of(k * yc, yc), yc), :]
 
-    pl.semaphore_wait(barrier, (nz - 1) + (nq - 1) + nq)
+    pl.semaphore_wait(barrier, (nz - 1) + nz + 2 * (nq - 1))
 
     w_f = push_group(nk, ydev, lambda d: f_ref.at[pl.ds(pl.multiple_of(yto(d) * yc, yc), yc)], fa.at[k], fa.at[pl.ds(0, nk - 1)])
     w_cs = chain_core(0)
+    w_zb = push_both(nz, zdev, zodev, lambda d: zb.at[p], lambda d: zb.at[p], zb.at[p],
+                     zb.at[pl.ds(0, nz - 1)], zb.at[pl.ds(0, nz)])
     w_w = push_group(nk, ydev, lambda d: wx.at[k], wx.at[k], wx.at[pl.ds(0, nk - 1)])
     w_cs()
     w_z = chain_z(0)
@@ -273,7 +281,15 @@
     gram_c = dot(ws, ws, 0, 0)
     w_f()
     g = dot(fa[...].reshape(ri, rj), shifted)
-    gw = add([g[i * yc:(i + 1) * yc] * ws[i:i + 1] for i in range(nk)])
+    here = [jnp.sum(fa[i], axis=1, keepdims=True) for i in range(nk)]
+    w_zb()
+    means = zb[:, 0, :]
+    mean = jnp.sum(means, axis=0, keepdims=True) / (2 * nz)
+    off = own - mean
+    moved = jnp.sum((means - mean) * zb[:, 1, :], axis=0, keepdims=True)
+    vs[0, :, :] = moved[:, 0:H]
+    vs[1, :, :] = moved[:, H:R]
+    gw = add([(g[i * yc:(i + 1) * yc] + here[i] * off) * ws[i:i + 1] for i in range(nk)])
     u[0, :, :] = gw[:, 0:H]
     u[1, :, :] = gw[:, H:R]
     def cut(h, zz):
@@ -392,7 +408,7 @@
     assert used[0] == NSEM
 
 
-NSEM = 22
+NSEM = 24
 PARTS = 4
 
 
@@ -435,6 +451,8 @@
             vm((nk, yc, rj)),
             vm((2, yc, H)),
             vm((yc, H)),
+            vm((2 * nz, 2, R)),
+            vm((2, 1, H)),
             vm((nz, yc // nz, H)),
             vm((2, yc, H)),
             vm((nq, 1, rj)),

time: 78.1 us -> 81 us (1.037)
  Pallas kernels: 77.3 us -> 80.2 us
    pallas_call x1, Pallas kernels: 75.4 us -> 78.3 us  [per_device(): pl.pallas_call(functools.partial(kernel, ne, nz, nk), out_shape=shapes, i...]
where the time goes in v7:
time: 81 us; the launch traced here: 80.9 us
  Pallas kernels  80.2 us (99%)
    pallas_call x1, Pallas kernels, per_device(): pl.pallas_call(functools.partial(kernel, ne, nz, nk), out_shape=shapes, i...  78.3 us
    pallas_call x1, Pallas kernels, per_device(): pl.pallas_call(hand_over, out_shape=shapes, in_specs=[pl.BlockSpec(memory...  1.93 us

profile of v7, /device:TPU:1, one launch (start us, length us, event | category | flops | bytes accessed | tf_op | source)
XLA Modules:
  0.0 80.9 jit_solution(1408679132443788148)
XLA Ops:
  0.6 78.3 %shard_map.58 = (f32[512,256]{1,0:T(8,128)}, f32[128,256]{1,0:T(8,128)}, f32[1,256]{1,0:T(1,128)}) custom-call(f32[1,512,128]{2,1,0:T(8,128)} %f_hbm.1, f32[128,256]{1,0:T(8,128)} %b_hbm.1, f32[1,256]{1,0:T(1,128)} %w_hbm.1), custom_call_target="tpu_custom_call" | custom-call | tf_op jit(solution)/shard_map/pallas_call | solution.py:442
  79.0 1.9 %shard_map.59 = (f32[512,256]{1,0:T(8,128)}, f32[128,256]{1,0:T(8,128)}, f32[1,256]{1,0:T(1,128)}) custom-call(f32[512,256]{1,0:T(8,128)} %get-tuple-element.6.a_in, f32[128,256]{1,0:T(8,128)} %get-tuple-element.7.b_in, f32[1,256]{1,0:T(1,128)} %get-tuple-element.8.c_in), custom_call_target="tpu_custom_call" | custom-call | tf_op jit(solution)/shard_map/pallas_call | solution.py:484

commit v8 on v7

--- a/solution.py
+++ b/solution.py
@@ -267,10 +267,10 @@
 
     pl.semaphore_wait(barrier, (nz - 1) + nz + 2 * (nq - 1))
 
+    w_zb = push_both(nz, zdev, zodev, lambda d: zb.at[p], lambda d: zb.at[p], zb.at[p],
+                     zb.at[pl.ds(0, nz - 1)], zb.at[pl.ds(0, nz)])
     w_f = push_group(nk, ydev, lambda d: f_ref.at[pl.ds(pl.multiple_of(yto(d) * yc, yc), yc)], fa.at[k], fa.at[pl.ds(0, nk - 1)])
     w_cs = chain_core(0)
-    w_zb = push_both(nz, zdev, zodev, lambda d: zb.at[p], lambda d: zb.at[p], zb.at[p],
-                     zb.at[pl.ds(0, nz - 1)], zb.at[pl.ds(0, nz)])
     w_w = push_group(nk, ydev, lambda d: wx.at[k], wx.at[k], wx.at[pl.ds(0, nk - 1)])
     w_cs()
     w_z = chain_z(0)

time: 81 us -> 81.6 us (level)
  no operation moved by 1% of the time
where the time goes in v8:
time: 81.6 us; the launch traced here: 81.4 us
  Pallas kernels  80.8 us (99%)
    pallas_call x1, Pallas kernels, per_device(): pl.pallas_call(functools.partial(kernel, ne, nz, nk), out_shape=shapes, i...  78.9 us
    pallas_call x1, Pallas kernels, per_device(): pl.pallas_call(hand_over, out_shape=shapes, in_specs=[pl.BlockSpec(memory...  1.93 us

profile of v8, /device:TPU:1, one launch (start us, length us, event | category | flops | bytes accessed | tf_op | source)
XLA Modules:
  0.0 81.4 jit_solution(14984243587104647330)
XLA Ops:
  0.6 78.9 %shard_map.58 = (f32[512,256]{1,0:T(8,128)}, f32[128,256]{1,0:T(8,128)}, f32[1,256]{1,0:T(1,128)}) custom-call(f32[1,512,128]{2,1,0:T(8,128)} %f_hbm.1, f32[128,256]{1,0:T(8,128)} %b_hbm.1, f32[1,256]{1,0:T(1,128)} %w_hbm.1), custom_call_target="tpu_custom_call" | custom-call | tf_op jit(solution)/shard_map/pallas_call | solution.py:442
  79.5 1.9 %shard_map.59 = (f32[512,256]{1,0:T(8,128)}, f32[128,256]{1,0:T(8,128)}, f32[1,256]{1,0:T(1,128)}) custom-call(f32[512,256]{1,0:T(8,128)} %get-tuple-element.6.a_in, f32[128,256]{1,0:T(8,128)} %get-tuple-element.7.b_in, f32[1,256]{1,0:T(1,128)} %get-tuple-element.8.c_in), custom_call_target="tpu_custom_call" | custom-call | tf_op jit(solution)/shard_map/pallas_call | solution.py:484
